TPU v7x, 128 devices: a whole 4x4x4 slice. The times are simulated.
128 devices in a mesh: dp: 8 (over z, core), ctx: 16 (over x, y).
Axes of the slice: x: 4, y: 4, z: 4, core: 2. Of those that a mesh axis runs over, the one named last changes fastest.
Arguments:
- query_rows: bfloat16 [16384, 4096], P(('dp', 'ctx')), may hold values from -8 to 8
- key_rows: bfloat16 [16384, 512], P(('dp', 'ctx')), may hold values from -8 to 8
- value_rows: bfloat16 [16384, 512], P(('dp', 'ctx')), may hold values from -6 to 6
- grad_out: bfloat16 [16384, 4096], P(('dp', 'ctx')), may hold values from -6 to 6
- send_order: int32 [8, 16, 128], P('dp', 'ctx'), may hold values from 0 to 127, each once within a row
- recv_place: int32 [8, 16, 128], P('dp', 'ctx'), may hold values from 0 to 127, each once within a row
- doc_ids: int32 [8, 2048], P('dp'), may hold values from 0 to 7, never falling along the last dimension, each value on 1 to 1024 neighbouring positions
Outputs:
- attn_out: bfloat16 [16384, 4096], P(('dp', 'ctx'))
- grad_queries: bfloat16 [16384, 4096], P(('dp', 'ctx'))
- grad_keys: bfloat16 [16384, 512], P(('dp', 'ctx'))
- grad_values: bfloat16 [16384, 512], P(('dp', 'ctx'))
Inputs may be any that keep to these rules, and one draw needn't show every extreme that they name: `send_order`: each row of a device is a permutation of its 128 slots. `recv_place`: each row of a device is a permutation of its 128 slots. `doc_ids`: never falling along a row; a document holds at most 1024 positions and one in each row holds exactly that many.
All inputs are finite; a program needn't handle non-finite values.
Results may differ from a plain program's by a relative error of at most 0.035.
Values may be sent and summed in bfloat16 or wider, within the bound.
A program may use at most 128 MiB of HBM per device.

v0:
```python
import math

import jax
import jax.numpy as jnp
from jax import lax
from jax.sharding import PartitionSpec as P

HEAD_DIM = 128


BIG_NEG = -1e30


def block_scores(query_heads, key_block, query_pos, query_doc, key_pos, key_doc, scaling):
    scores = (
        jnp.einsum("rkgd,jkd->kgrj", query_heads, key_block, preferred_element_type=jnp.float32)
        * scaling
    )
    allowed = (query_doc[:, None] == key_doc[None, :]) & (key_pos[None, :] <= query_pos[:, None])
    return (scores, allowed)


def stats_update(running, scores, allowed):
    run_max, run_sum = running
    block_max = jnp.max(jnp.where(allowed, scores, BIG_NEG), axis=-1)
    new_max = jnp.maximum(run_max, block_max)
    weights = jnp.where(allowed, jnp.exp(scores - new_max[..., None]), 0.0)
    return (new_max, run_sum * jnp.exp(run_max - new_max) + jnp.sum(weights, axis=-1))


def output_term(scores, allowed, log_total, value_block):
    weights = jnp.where(allowed, jnp.exp(scores - log_total[..., None]), 0.0)
    return jnp.einsum(
        "kgrj,jkd->rkgd",
        weights.astype(jnp.bfloat16),
        value_block,
        preferred_element_type=jnp.float32,
    )


def grad_terms(
    scores, allowed, log_total, row_delta, query_heads, grad_heads, key_block, value_block, scaling
):
    weights = jnp.where(allowed, jnp.exp(scores - log_total[..., None]), 0.0)
    prob_grad = jnp.einsum(
        "rkgd,jkd->kgrj", grad_heads, value_block, preferred_element_type=jnp.float32
    )
    dscore = (weights * (prob_grad - row_delta[..., None])).astype(jnp.bfloat16)
    query_term = jnp.einsum("kgrj,jkd->rkgd", dscore, key_block, preferred_element_type=jnp.float32)
    key_term = (
        jnp.einsum("kgrj,rkgd->jkd", dscore, query_heads, preferred_element_type=jnp.float32)
        * scaling
    )
    value_term = jnp.einsum(
        "kgrj,rkgd->jkd",
        weights.astype(jnp.bfloat16),
        grad_heads,
        preferred_element_type=jnp.float32,
    )
    return (query_term, key_term, value_term)


def body(query_rows, key_rows, value_rows, grad_out, send_order, recv_place, doc_ids):
    tok_rows = query_rows.shape[0]
    ctx_count = lax.axis_size("ctx")
    ctx_index = lax.axis_index("ctx")
    seq_len = tok_rows * ctx_count
    kv_heads = key_rows.shape[1] // HEAD_DIM
    group_size = query_rows.shape[1] // key_rows.shape[1]
    scaling = HEAD_DIM ** (-0.5)
    order_row = send_order.reshape(tok_rows)
    place_row = recv_place.reshape(tok_rows)
    counting = jnp.arange(tok_rows, dtype=jnp.int32)
    place_inverse = jnp.zeros((tok_rows,), jnp.int32).at[place_row].set(counting)
    order_inverse = jnp.zeros((tok_rows,), jnp.int32).at[order_row].set(counting)
    arrived = (
        lax.all_to_all(query_rows[order_row], "dp", split_axis=0, concat_axis=0, tiled=True),
        lax.all_to_all(key_rows[order_row], "dp", split_axis=0, concat_axis=0, tiled=True),
        lax.all_to_all(value_rows[order_row], "dp", split_axis=0, concat_axis=0, tiled=True),
        lax.all_to_all(grad_out[order_row], "dp", split_axis=0, concat_axis=0, tiled=True),
    )
    query_att, key_att, value_att, grad_att = [member[place_inverse] for member in arrived]
    doc_row = doc_ids.reshape(seq_len)
    query_pos = ctx_index * tok_rows + counting
    query_doc = lax.dynamic_slice_in_dim(doc_row, ctx_index * tok_rows, tok_rows)
    query_heads = query_att.reshape(tok_rows, kv_heads, group_size, HEAD_DIM)
    grad_heads = grad_att.reshape(tok_rows, kv_heads, group_size, HEAD_DIM)
    key_local = key_att.reshape(tok_rows, kv_heads, HEAD_DIM)
    value_local = value_att.reshape(tok_rows, kv_heads, HEAD_DIM)
    stat_shape = (kv_heads, group_size, tok_rows)
    start_stats = (jnp.full(stat_shape, BIG_NEG, jnp.float32), jnp.zeros(stat_shape, jnp.float32))
    zero_query = jnp.zeros((tok_rows, kv_heads, group_size, HEAD_DIM), jnp.float32)
    whole_key, whole_value = (
        lax.all_gather(key_local, "ctx", axis=0, tiled=True),
        lax.all_gather(value_local, "ctx", axis=0, tiled=True),
    )
    block_len = math.gcd(seq_len, 512)
    block_count = seq_len // block_len
    key_blocks = whole_key.reshape(block_count, block_len, kv_heads, HEAD_DIM)
    value_blocks = whole_value.reshape(block_count, block_len, kv_heads, HEAD_DIM)
    pos_blocks = jnp.arange(seq_len, dtype=jnp.int32).reshape(block_count, block_len)
    doc_blocks = doc_row.reshape(block_count, block_len)
    block_inputs = (key_blocks, value_blocks, pos_blocks, doc_blocks)

    def stats_step(running, inputs):
        scores, allowed = block_scores(
            query_heads, inputs[0], query_pos, query_doc, inputs[2], inputs[3], scaling
        )
        return (stats_update(running, scores, allowed), None)

    (run_max, run_sum), unused = lax.scan(stats_step, start_stats, block_inputs)
    log_total = run_max + jnp.log(run_sum)

    def out_step(so_far, inputs):
        scores, allowed = block_scores(
            query_heads, inputs[0], query_pos, query_doc, inputs[2], inputs[3], scaling
        )
        return (so_far + output_term(scores, allowed, log_total, inputs[1]), None)

    out_sum, unused = lax.scan(out_step, zero_query, block_inputs)
    attn_att = out_sum.reshape(tok_rows, -1).astype(jnp.bfloat16)
    out_back = lax.all_to_all(attn_att[place_row], "dp", split_axis=0, concat_axis=0, tiled=True)
    out_heads = attn_att.reshape(tok_rows, kv_heads, group_size, HEAD_DIM)
    row_delta = jnp.sum(
        grad_heads.astype(jnp.float32) * out_heads.astype(jnp.float32), axis=-1
    ).transpose(1, 2, 0)

    def grad_step(so_far, inputs):
        scores, allowed = block_scores(
            query_heads, inputs[0], query_pos, query_doc, inputs[2], inputs[3], scaling
        )
        query_term, key_term, value_term = grad_terms(
            scores,
            allowed,
            log_total,
            row_delta,
            query_heads,
            grad_heads,
            inputs[0],
            inputs[1],
            scaling,
        )
        return (so_far + query_term, (key_term, value_term))

    query_sum, (key_parts, value_parts) = lax.scan(grad_step, zero_query, block_inputs)
    key_mine, value_mine = (
        lax.psum_scatter(key_parts.reshape(seq_len, -1), "ctx", scatter_dimension=0, tiled=True),
        lax.psum_scatter(value_parts.reshape(seq_len, -1), "ctx", scatter_dimension=0, tiled=True),
    )
    grad_q_att = (query_sum * scaling).reshape(tok_rows, -1).astype(jnp.bfloat16)
    grad_k_att = key_mine.astype(jnp.bfloat16)
    grad_v_att = value_mine.astype(jnp.bfloat16)
    grads_back = (
        lax.all_to_all(grad_q_att[place_row], "dp", split_axis=0, concat_axis=0, tiled=True),
        lax.all_to_all(grad_k_att[place_row], "dp", split_axis=0, concat_axis=0, tiled=True),
        lax.all_to_all(grad_v_att[place_row], "dp", split_axis=0, concat_axis=0, tiled=True),
    )
    all_back = (out_back, grads_back[0], grads_back[1], grads_back[2])
    return tuple((member[order_inverse] for member in all_back))


def solution(mesh):
    placed = (
        P(("dp", "ctx"), None),
        P(("dp", "ctx"), None),
        P(("dp", "ctx"), None),
        P(("dp", "ctx"), None),
        P("dp", "ctx", None),
        P("dp", "ctx", None),
        P("dp", None),
    )
    return jax.shard_map(
        body,
        mesh=mesh,
        in_specs=placed,
        out_specs=(
            P(("dp", "ctx"), None),
            P(("dp", "ctx"), None),
            P(("dp", "ctx"), None),
            P(("dp", "ctx"), None),
        ),
        check_vma=False,
    )
```

profile of v0, /device:TPU:1, one launch (start us, length us, event | category | flops | bytes accessed | tf_op | source)
XLA Modules:
  0.0 396.9 jit_solution(7387957839080141849)
XLA Ops:
  8.5 2.4 gather_fusion.2
  11.0 6.8 %all-to-all-start.1 = ((bf16[8,16,512]{2,1,0:T(8,128)(2,1)}), bf16[8,16,512]{2,1,0:T(8,128)(2,1)S(1)}, u32[]{:S(2)}, u32[]{:S(2)}) async-start(bf16[8,16,512]{2,1,0:T(8,128)(2,1)} %bitcast.8), calls=%async_computation.1 | async-start | bytes 262144 | tf_op jit(solution)/shard_map/all_to_all | solution.py:78
  19.4 3.6 all-to-all-done.1
  24.6 2.5 gather_fusion
  27.1 4.1 %all-to-all-start = ((bf16[8,16,512]{2,1,0:T(8,128)(2,1)}), bf16[8,16,512]{2,1,0:T(8,128)(2,1)S(1)}, u32[]{:S(2)}, u32[]{:S(2)}) async-start(bf16[8,16,512]{2,1,0:T(8,128)(2,1)} %bitcast.2), calls=%async_computation | async-start | bytes 262144 | tf_op jit(solution)/shard_map/all_to_all | solution.py:79
  31.2 2.2 gather_fusion.8
  33.4 3.1 all-to-all-done
  36.5 4.3 %all-to-all-start.4 = ((bf16[8,16,4096]{2,1,0:T(8,128)(2,1)}), bf16[8,16,4096]{2,1,0:T(8,128)(2,1)S(1)}, u32[]{:S(2)}, u32[]{:S(2)}) async-start(bf16[8,16,4096]{2,1,0:T(8,128)(2,1)} %bitcast.251), calls=%async_computation.4 | async-start | bytes 2097152 | tf_op jit(solution)/shard_map/all_to_all | solution.py:80
  40.8 2.2 gather_fusion.4
  43.0 12.9 %all-to-all-done.4 = bf16[8,16,4096]{2,1,0:T(8,128)(2,1)S(1)} async-done(((bf16[8,16,4096]{2,1,0:T(8,128)(2,1)}), bf16[8,16,4096]{2,1,0:T(8,128)(2,1)S(1)}, u32[]{:S(2)}, u32[]{:S(2)}) %all-to-all-start.4) | async-done | bytes 1048608 | tf_op jit(solution)/shard_map/all_to_all | solution.py:80
  55.9 4.3 %all-to-all-start.2 = ((bf16[8,16,4096]{2,1,0:T(8,128)(2,1)}), bf16[8,16,4096]{2,1,0:T(8,128)(2,1)S(1)}, u32[]{:S(2)}, u32[]{:S(2)}) async-start(bf16[8,16,4096]{2,1,0:T(8,128)(2,1)} %bitcast.249), calls=%async_computation.2 | async-start | bytes 2097152 | tf_op jit(solution)/shard_map/all_to_all | solution.py:77
  64.8 1.4 copy.36
  66.2 1.7 copy.32
  67.9 7.5 %all-to-all-done.2 = bf16[8,16,4096]{2,1,0:T(8,128)(2,1)S(1)} async-done(((bf16[8,16,4096]{2,1,0:T(8,128)(2,1)}), bf16[8,16,4096]{2,1,0:T(8,128)(2,1)S(1)}, u32[]{:S(2)}, u32[]{:S(2)}) %all-to-all-start.2) | async-done | bytes 1048608 | tf_op jit(solution)/shard_map/all_to_all | solution.py:77
  78.2 1.7 copy.27
  80.0 13.5 %while.39 = (s32[]{:T(128)}, f32[4,8,128]{2,1,0:T(8,128)S(1)}, f32[4,8,128]{2,1,0:T(8,128)S(1)}, s32[128]{0:T(128)S(1)}, s32[4,512]{1,0:T(4,128)S(1)}, /*index=5...) while((s32[]{:T(128)}, f32[4,8,128]{2,1,0:T(8,128)S(1)}, ...), condition=%wide.region_4.5_spmd.clone, body=%wide.region_1.4_spmd.clone.sunk | while | flops 551768192 | bytes 18773644 | solution.py:111
  81.6 1.8 fusion.101
  84.9 1.8 fusion.101
  88.3 1.8 fusion.101
  91.7 1.8 fusion.101
  93.5 21.9 %all-gather.3.cloned.1.call-done = bf16[2048,4,128]{2,0,1:T(8,128)(2,1)} async-done(((bf16[128,4,128]{2,0,1:T(8,128)(2,1)}), bf16[2048,4,128]{2,0,1:T(8,128)(2,1)}) %all-gather.3.cloned.1.call-update) | async-done | bytes 2097168 | tf_op jit(solution)/shard_map/all_gather | solution.py:95
  115.4 37.1 %while.40 = (s32[]{:T(128)}, f32[128,4,8,128]{0,3,2,1:T(8,128)}, bf16[4,512,4,128]{3,1,0,2:T(8,128)(2,1)}, s32[128]{0:T(128)S(1)}, s32[4,512]{1,0:T(4,128)S(1)},...) while((s32[]{:T(128)}, f32[128,4,8,128]{0,3,2,1:T(8,128)}, ...), condition=%wide.region_6.7_spmd.clone, body=%wide.region_5.6_spmd.clone.sunk | while | flops 1083375744 | bytes 8550039 | solution.py:120
  117.8 6.3 %bitcast_add_fusion.4 = f32[128,4,8,128]{0,3,2,1:T(8,128)} fusion(f32[128,4,8,128]{0,3,2,1:T(8,128)} %get-tuple-element.706, f32[4,8,128]{2,1,0:T(8,128)S(1)} %get-tuple-element.725, pred[128,512]{1,0:T(8,128)(4,1)S(1)} %compare_and_fusion.7, bf16[128,4,8,128]{3,2,1,0:T(8,128)(2,1)} %get-tuple-element.724, pred[]{:T(512)S(6)} %compare.10, ...), kind=kOutput, calls=%fused_computation.48.clone.1 | convolution fusion | flops 1083179008 | bytes 6373381 | tf_op jit(solution)/shard_map/while/body/eval_jaxpr/kgrj,jkd->rkgd/dot_general | solution.py:33
  126.6 7.0 %bitcast_add_fusion.4 = f32[128,4,8,128]{0,3,2,1:T(8,128)} fusion(f32[128,4,8,128]{0,3,2,1:T(8,128)} %get-tuple-element.706, f32[4,8,128]{2,1,0:T(8,128)S(1)} %get-tuple-element.725, pred[128,512]{1,0:T(8,128)(4,1)S(1)} %compare_and_fusion.7, bf16[128,4,8,128]{3,2,1,0:T(8,128)(2,1)} %get-tuple-element.724, pred[]{:T(512)S(6)} %compare.10, ...), kind=kOutput, calls=%fused_computation.48.clone.1 | convolution fusion | flops 1083179008 | bytes 6373381 | tf_op jit(solution)/shard_map/while/body/eval_jaxpr/kgrj,jkd->rkgd/dot_general | solution.py:33
  136.0 7.0 %bitcast_add_fusion.4 = f32[128,4,8,128]{0,3,2,1:T(8,128)} fusion(f32[128,4,8,128]{0,3,2,1:T(8,128)} %get-tuple-element.706, f32[4,8,128]{2,1,0:T(8,128)S(1)} %get-tuple-element.725, pred[128,512]{1,0:T(8,128)(4,1)S(1)} %compare_and_fusion.7, bf16[128,4,8,128]{3,2,1,0:T(8,128)(2,1)} %get-tuple-element.724, pred[]{:T(512)S(6)} %compare.10, ...), kind=kOutput, calls=%fused_computation.48.clone.1 | convolution fusion | flops 1083179008 | bytes 6373381 | tf_op jit(solution)/shard_map/while/body/eval_jaxpr/kgrj,jkd->rkgd/dot_general | solution.py:33
  145.5 7.0 %bitcast_add_fusion.4 = f32[128,4,8,128]{0,3,2,1:T(8,128)} fusion(f32[128,4,8,128]{0,3,2,1:T(8,128)} %get-tuple-element.706, f32[4,8,128]{2,1,0:T(8,128)S(1)} %get-tuple-element.725, pred[128,512]{1,0:T(8,128)(4,1)S(1)} %compare_and_fusion.7, bf16[128,4,8,128]{3,2,1,0:T(8,128)(2,1)} %get-tuple-element.724, pred[]{:T(512)S(6)} %compare.10, ...), kind=kOutput, calls=%fused_computation.48.clone.1 | convolution fusion | flops 1083179008 | bytes 6373381 | tf_op jit(solution)/shard_map/while/body/eval_jaxpr/kgrj,jkd->rkgd/dot_general | solution.py:33
  152.5 3.4 multiply_reduce_fusion
  155.9 56.5 %while.41 = (s32[]{:T(128)}, f32[128,4,8,128]{0,3,2,1:T(8,128)S(1)}, f32[4,512,4,128]{3,2,1,0:T(4,128)}, f32[4,512,4,128]{3,2,1,0:T(4,128)}, bf16[4,512,4,128]{3...) while((s32[]{:T(128)}, ...), condition=%wide.region_10.11_spmd.clone, body=%wide.region_9.10_spmd.clone.sunk | while | flops 2706833408 | bytes 58455772 | solution.py:145
  156.2 2.4 fusion.117
  160.0 3.8 fusion.118
  165.0 2.3 bitcast_add_fusion.5
  167.4 2.7 copy_dynamic-update-slice_fusion.3
  170.3 2.4 fusion.117
  172.7 1.4 fusion.119
  174.1 3.8 fusion.118
  179.2 2.3 bitcast_add_fusion.5
  181.5 2.6 copy_dynamic-update-slice_fusion.3
  184.4 2.4 fusion.117
  188.2 3.8 fusion.118
  193.3 2.3 bitcast_add_fusion.5
  195.6 2.7 copy_dynamic-update-slice_fusion.3
  198.5 2.4 fusion.117
  202.3 3.8 fusion.118
  207.4 2.3 bitcast_add_fusion.5
  209.7 2.7 copy_dynamic-update-slice_fusion.3
  212.4 4.6 %copy.82 = f32[256,8,4,128]{3,1,2,0:T(8,128)} copy(f32[256,8,4,128]{3,2,1,0:T(4,128)} %bitcast.255) | data formatting | bytes 8388608
  217.1 4.6 %copy.83 = f32[256,8,4,128]{3,1,2,0:T(8,128)} copy(f32[256,8,4,128]{3,2,1,0:T(4,128)} %bitcast.256) | data formatting | bytes 8388608
  222.4 1.5 copy.50
  223.8 2.2 gather_fusion.6
  226.0 5.9 %all-to-all-start.3 = ((bf16[8,16,4096]{2,1,0:T(8,128)(2,1)}), bf16[8,16,4096]{2,1,0:T(8,128)(2,1)S(1)}, u32[]{:S(2)}, u32[]{:S(2)}) async-start(bf16[8,16,4096]{2,1,0:T(8,128)(2,1)} %bitcast.250), calls=%async_computation.3 | async-start | bytes 2097152 | tf_op jit(solution)/shard_map/all_to_all | solution.py:122
  233.2 1.5 copy.51
  234.7 2.2 gather_fusion.10
  236.8 10.2 %all-to-all-done.3 = bf16[8,16,4096]{2,1,0:T(8,128)(2,1)S(1)} async-done(((bf16[8,16,4096]{2,1,0:T(8,128)(2,1)}), bf16[8,16,4096]{2,1,0:T(8,128)(2,1)S(1)}, u32[]{:S(2)}, u32[]{:S(2)}) %all-to-all-start.3) | async-done | bytes 1048608 | tf_op jit(solution)/shard_map/all_to_all | solution.py:122
  247.0 4.3 %all-to-all-start.5 = ((bf16[8,16,4096]{2,1,0:T(8,128)(2,1)}), bf16[8,16,4096]{2,1,0:T(8,128)(2,1)S(1)}, u32[]{:S(2)}, u32[]{:S(2)}) async-start(bf16[8,16,4096]{2,1,0:T(8,128)(2,1)} %bitcast.20), calls=%async_computation.5 | async-start | bytes 2097152 | tf_op jit(solution)/shard_map/all_to_all | solution.py:154
  251.4 41.9 %reduce-scatter.5.cloned.1.call-done = f32[128,512]{1,0:T(8,128)} async-done(((f32[2048,512]{1,0:T(8,128)}), f32[128,512]{1,0:T(8,128)}) %reduce-scatter.5.cloned.1.call-update) | async-done | bytes 262160 | tf_op jit(solution)/shard_map/reduce_scatter | solution.py:148
  294.3 1.5 gather_fusion.14
  295.8 6.7 %all-to-all-start.7 = ((bf16[8,16,512]{2,1,0:T(8,128)(2,1)}), bf16[8,16,512]{2,1,0:T(8,128)(2,1)S(1)}, u32[]{:S(2)}, u32[]{:S(2)}) async-start(bf16[8,16,512]{2,1,0:T(8,128)(2,1)} %bitcast.24), calls=%async_computation.9 | async-start | bytes 262144 | tf_op jit(solution)/shard_map/all_to_all | solution.py:156
  303.9 69.9 %reduce-scatter.3.cloned.1.call-done = f32[128,512]{1,0:T(8,128)} async-done(((f32[2048,512]{1,0:T(8,128)}), f32[128,512]{1,0:T(8,128)}) %reduce-scatter.3.cloned.1.call-update) | async-done | bytes 262160 | tf_op jit(solution)/shard_map/reduce_scatter | solution.py:147
  374.8 1.5 gather_fusion.12
  376.3 6.8 %all-to-all-start.6 = ((bf16[8,16,512]{2,1,0:T(8,128)(2,1)}), bf16[8,16,512]{2,1,0:T(8,128)(2,1)S(1)}, u32[]{:S(2)}, u32[]{:S(2)}) async-start(bf16[8,16,512]{2,1,0:T(8,128)(2,1)} %bitcast.22), calls=%async_computation.7 | async-start | bytes 262144 | tf_op jit(solution)/shard_map/all_to_all | solution.py:155
  383.0 2.2 gather_fusion.7
  385.2 2.2 gather_fusion.11
  387.4 1.5 gather_fusion.15
  388.9 1.5 gather_fusion.13
  (147 shorter events, 43.0 us)
Async XLA Ops:
  7.2 24.0 %copy-start = (bf16[128,4096]{1,0:T(8,128)(2,1)S(1)}, bf16[128,4096]{1,0:T(8,128)(2,1)}, u32[]{:S(2)}) copy-start(bf16[128,4096]{1,0:T(8,128)(2,1)} %param.16) | copy-start | bytes 3145732
  7.9 0.6 copy-start.8
  11.0 12.1 %all-to-all-start.1 = ((bf16[8,16,512]{2,1,0:T(8,128)(2,1)}), bf16[8,16,512]{2,1,0:T(8,128)(2,1)S(1)}, u32[]{:S(2)}, u32[]{:S(2)}) async-start(bf16[8,16,512]{2,1,0:T(8,128)(2,1)} %bitcast.8), calls=%async_computation.1 | async-start | bytes 262144 | tf_op jit(solution)/shard_map/all_to_all | solution.py:78
  17.8 60.5 %all-gather.5.cloned.1.call-start = ((), (), s32[]{:S(2)}) async-start(), calls=%async_computation.11 | async-start | bytes 2228224 | tf_op jit(solution)/shard_map/all_gather | solution.py:94
  18.4 4.6 %copy-start.9 = (s32[128]{0:T(128)}, s32[128]{0:T(128)S(1)}, u32[]{:S(2)}) copy-start(s32[128]{0:T(128)S(1)} %fusion.63) | copy-start | bytes 1540
  27.1 9.4 %all-to-all-start = ((bf16[8,16,512]{2,1,0:T(8,128)(2,1)}), bf16[8,16,512]{2,1,0:T(8,128)(2,1)S(1)}, u32[]{:S(2)}, u32[]{:S(2)}) async-start(bf16[8,16,512]{2,1,0:T(8,128)(2,1)} %bitcast.2), calls=%async_computation | async-start | bytes 262144 | tf_op jit(solution)/shard_map/all_to_all | solution.py:79
  31.2 9.6 %copy-start.3 = (bf16[128,4096]{1,0:T(8,128)(2,1)S(1)}, bf16[128,4096]{1,0:T(8,128)(2,1)}, u32[]{:S(2)}) copy-start(bf16[128,4096]{1,0:T(8,128)(2,1)} %param.13) | copy-start | bytes 3145732
  36.5 19.4 %all-to-all-start.4 = ((bf16[8,16,4096]{2,1,0:T(8,128)(2,1)}), bf16[8,16,4096]{2,1,0:T(8,128)(2,1)S(1)}, u32[]{:S(2)}, u32[]{:S(2)}) async-start(bf16[8,16,4096]{2,1,0:T(8,128)(2,1)} %bitcast.251), calls=%async_computation.4 | async-start | bytes 2097152 | tf_op jit(solution)/shard_map/all_to_all | solution.py:80
  40.8 20.0 %copy-start.7 = (s32[1,2048]{1,0:T(1,128)S(1)}, s32[1,2048]{1,0:T(1,128)}, u32[]{:S(2)}) copy-start(s32[1,2048]{1,0:T(1,128)} %param.19) | copy-start | bytes 24580
  55.9 19.5 %all-to-all-start.2 = ((bf16[8,16,4096]{2,1,0:T(8,128)(2,1)}), bf16[8,16,4096]{2,1,0:T(8,128)(2,1)S(1)}, u32[]{:S(2)}, u32[]{:S(2)}) async-start(bf16[8,16,4096]{2,1,0:T(8,128)(2,1)} %bitcast.249), calls=%async_computation.2 | async-start | bytes 2097152 | tf_op jit(solution)/shard_map/all_to_all | solution.py:77
  60.3 55.1 %all-gather.3.cloned.1.call-start = ((), (), s32[]{:S(2)}) async-start(), calls=%async_computation.10 | async-start | bytes 2228224 | tf_op jit(solution)/shard_map/all_gather | solution.py:95
  63.1 230.2 %reduce-scatter.5.cloned.1.call-start = ((), (), s32[]{:S(2)}) async-start(), calls=%async_computation.13 | async-start | bytes 4456448 | tf_op jit(solution)/shard_map/reduce_scatter | solution.py:148
  76.8 1.0 copy-start.5
  93.5 21.9 %copy-start.4 = (bf16[4,512,4,128]{3,1,2,0:T(8,128)(2,1)}, bf16[4,512,4,128]{3,1,2,0:T(8,128)(2,1)S(1)}, u32[]{:S(2)}) copy-start(bf16[4,512,4,128]{3,1,2,0:T(8,128)(2,1)S(1)} %get-tuple-element.786) | copy-start | bytes 6291460
  152.5 3.4 copy-start.2
  156.2 2.4 copy-start.6
  170.3 2.4 copy-start.6
  184.4 2.4 copy-start.6
  198.5 2.4 copy-start.6
  217.1 156.7 %reduce-scatter.3.cloned.1.call-start = ((), (), s32[]{:S(2)}) async-start(), calls=%async_computation.12 | async-start | bytes 4456448 | tf_op jit(solution)/shard_map/reduce_scatter | solution.py:147
  221.8 0.6 copy-start.10
  226.0 21.0 %all-to-all-start.3 = ((bf16[8,16,4096]{2,1,0:T(8,128)(2,1)}), bf16[8,16,4096]{2,1,0:T(8,128)(2,1)S(1)}, u32[]{:S(2)}, u32[]{:S(2)}) async-start(bf16[8,16,4096]{2,1,0:T(8,128)(2,1)} %bitcast.250), calls=%async_computation.3 | async-start | bytes 2097152 | tf_op jit(solution)/shard_map/all_to_all | solution.py:122
  247.0 48.7 %all-to-all-start.5 = ((bf16[8,16,4096]{2,1,0:T(8,128)(2,1)}), bf16[8,16,4096]{2,1,0:T(8,128)(2,1)S(1)}, u32[]{:S(2)}, u32[]{:S(2)}) async-start(bf16[8,16,4096]{2,1,0:T(8,128)(2,1)} %bitcast.20), calls=%async_computation.5 | async-start | bytes 2097152 | tf_op jit(solution)/shard_map/all_to_all | solution.py:154
  295.8 80.5 %all-to-all-start.7 = ((bf16[8,16,512]{2,1,0:T(8,128)(2,1)}), bf16[8,16,512]{2,1,0:T(8,128)(2,1)S(1)}, u32[]{:S(2)}, u32[]{:S(2)}) async-start(bf16[8,16,512]{2,1,0:T(8,128)(2,1)} %bitcast.24), calls=%async_computation.9 | async-start | bytes 262144 | tf_op jit(solution)/shard_map/all_to_all | solution.py:156
  376.3 12.6 %all-to-all-start.6 = ((bf16[8,16,512]{2,1,0:T(8,128)(2,1)}), bf16[8,16,512]{2,1,0:T(8,128)(2,1)S(1)}, u32[]{:S(2)}, u32[]{:S(2)}) async-start(bf16[8,16,512]{2,1,0:T(8,128)(2,1)} %bitcast.22), calls=%async_computation.7 | async-start | bytes 262144 | tf_op jit(solution)/shard_map/all_to_all | solution.py:155
  385.2 5.2 %copy-start.1 = (bf16[128,4096]{1,0:T(8,128)(2,1)S(1)}, bf16[128,4096]{1,0:T(8,128)(2,1)}, u32[]{:S(2)}) copy-start(bf16[128,4096]{1,0:T(8,128)(2,1)} %param.16) | copy-start | bytes 3145732
Sparse Core Ops, SparseCore 0:
  24.7 43.6 all-gather.4
  71.2 44.1 all-gather.2
  217.2 76.0 reduce-scatter.4
  296.9 76.8 reduce-scatter.2
where the time goes:
time: 399 us; the launch traced here: 397 us
  waiting for transfers between devices  171 us (43%)
  matrix products  77.2 us (19%)
  local copies, waits for them, and re-layouts  72.2 us (18%)
  starting transfers between devices  43.6 us (11%)
  other arithmetic  18 us (5%)
  between operations  14 us (4%)
    reduce_scatter x1, waiting for transfers between devices, body(): lax.psum_scatter(key_parts.reshape(seq_len, -1), 'ctx', scatter_dimension...  69.9 us
    reduce_scatter x1, waiting for transfers between devices, body(): lax.psum_scatter(value_parts.reshape(seq_len, -1), 'ctx', scatter_dimensi...  41.9 us
    dot_general x4, matrix products, output_term(): jnp.einsum('kgrj,jkd->rkgd', weights.astype(jnp.bfloat16), value_block, p...  27.3 us
    all_gather x1, waiting for transfers between devices, body(): lax.all_gather(value_local, 'ctx', axis=0, tiled=True)  21.9 us
    unnamed x28, local copies, waits for them, and re-layouts  15.9 us
    dot_general x4, matrix products, grad_terms(): jnp.einsum('rkgd,jkd->kgrj', grad_heads, value_block, preferred_element_t...  15.1 us
    dot_general x8, matrix products, block_scores(): jnp.einsum('rkgd,jkd->kgrj', query_heads, key_block, preferred_element_ty...  14.7 us
    all_to_all x1, waiting for transfers between devices, body(): lax.all_to_all(grad_out[order_row], 'dp', split_axis=0, concat_axis=0, ti...  12.9 us
  transfers between devices with their start and end apart: 12, of which 8 were waited for; matrix products, arithmetic and copies ran while one was open for 15% of the time, Pallas kernels for 0%

commit v1 on v0

v1 whole, which is shorter than its diff:
```python
import jax
import jax.numpy as jnp
from jax import lax
from jax.experimental import pallas as pl
from jax.experimental.pallas import tpu as pltpu
from jax.sharding import PartitionSpec as P

BF, F32, I32 = jnp.bfloat16, jnp.float32, jnp.int32
MESH = pl.DeviceIdType.MESH
HD = 128
KH = 4
GS = 8
T = 128
NDP = 8
SHARE = T // NDP
NCH = 9
W = NCH * T
GW = GS * HD
SCALE = HD**-0.5
SCALE2 = SCALE * 1.4426950408889634
NEG = -1e30
NT = (((1,), (1,)), ((), ()))
NN = (((1,), (0,)), ((), ()))


def dot(a, b, dims=NN):
    return lax.dot_general(a, b, dims, preferred_element_type=F32)


def kernel(
    q_hbm, k_hbm, v_hbm, g_hbm, order_ref, place_ref, doc_ref,
    out_hbm, dq_hbm, dk_hbm, dv_hbm,
    q_in, g_in, k_in, v_in, hot, hot_t, nat, nat_t,
    kvs, kvr, qgs, qgr, kv, bias, kt, vt,
    ods, odr, dkv, yrec, acc, xs, xrec, zks, zkr, home, gk, gv,
    in_sem, out_sem, kv_ss, kv_rs, qg_ss, qg_rs, x_ss, x_rs, y_ss, y_rs,
    od_ss, od_rs, yr_ss, yr_rs, xr_ss, xr_rs, zk_ss, zk_rs,
):
    d = lax.axis_index("dp")
    c = lax.axis_index("ctx")
    x, y = c // 4, c % 4

    def group_at(j):
        return (lax.rem(d + j, NDP), c)

    def x_at(j):
        return (d, lax.rem(x + j + 4, 4) * 4 + y)

    def y_at(j):
        return (d, x * 4 + lax.rem(y + j + 4, 4))

    bar = pltpu.get_barrier_semaphore()
    friends = [group_at(j) for j in range(1, NDP)]
    friends += [x_at(j) for j in range(1, 4)] + [y_at(j) for j in range(1, 4)]
    for f in friends:
        pl.semaphore_signal(bar, 1, device_id=f, device_id_type=MESH)

    k_cp = pltpu.make_async_copy(k_hbm, k_in, in_sem.at[0])
    v_cp = pltpu.make_async_copy(v_hbm, v_in, in_sem.at[1])
    q_cp = pltpu.make_async_copy(q_hbm, q_in, in_sem.at[2])
    g_cp = pltpu.make_async_copy(g_hbm, g_in, in_sem.at[3])
    for cp in (k_cp, v_cp, q_cp, g_cp):
        cp.start()

    rows = lax.broadcasted_iota(I32, (T, T), 0)
    hot_t32 = (rows == order_ref[...]).astype(F32)
    nat32 = (rows == place_ref[...]).astype(F32)
    hot_t[...] = hot_t32.astype(BF)
    hot[...] = hot_t32.T.astype(BF)
    nat[...] = nat32.astype(BF)
    nat_t[...] = nat32.T.astype(BF)

    mine = pl.ds(pl.multiple_of(d * SHARE, SHARE), SHARE)

    def part(j):
        return pl.ds(pl.multiple_of(lax.rem(d + j, NDP) * SHARE, SHARE), SHARE)

    def rcopy(src, dst, ss, rs, to):
        return pltpu.make_async_remote_copy(
            src_ref=src, dst_ref=dst, send_sem=ss, recv_sem=rs, device_id=to, device_id_type=MESH
        )

    def kv_copy(j):
        return rcopy(kvs.at[part(j)], kvr.at[mine], kv_ss.at[j], kv_rs.at[j], group_at(j))

    def qg_copy(g, j):
        return rcopy(
            qgs.at[g, part(j)], qgr.at[g, mine], qg_ss.at[g, j], qg_rs.at[g, j], group_at(j)
        )

    def od_copy(g, j):
        return rcopy(
            ods.at[g, part(j)], odr.at[g, mine], od_ss.at[g, j], od_rs.at[g, j], group_at(j)
        )

    def zk_copy(g, j):
        return rcopy(
            zks.at[g, part(j)], zkr.at[g, mine], zk_ss.at[g, j], zk_rs.at[g, j], group_at(j)
        )

    def chunk(o):
        return pl.ds(pl.multiple_of(o * T, T), T)

    def x_copy(g, j):
        return rcopy(
            kv.at[g, chunk(0)], kv.at[g, chunk(4 * j)], x_ss.at[g, j], x_rs.at[g, j], x_at(j)
        )

    def y_copy(g, j, b):
        turn = (y + j) // 4
        return rcopy(
            kv.at[g, chunk(4 * (turn + b))], kv.at[g, chunk(j + 4 * b)],
            y_ss.at[g, j, b], y_rs.at[g, j, b], y_at(j),
        )

    def yr_copy(g, j, b):
        return rcopy(
            dkv.at[g, chunk(j + 4 * b)], yrec.at[g, j - 1, b],
            yr_ss.at[g, j, b], yr_rs.at[g, j, b], y_at(-j),
        )

    def xr_copy(g, j):
        return rcopy(
            xs.at[g, j - 1], xrec.at[g, j - 1], xr_ss.at[g, j], xr_rs.at[g, j], x_at(-j)
        )

    k_cp.wait()
    v_cp.wait()
    for g in range(KH):
        cols = slice(g * HD, (g + 1) * HD)
        kvs[:, 2 * g * HD : (2 * g + 1) * HD] = dot(hot[...], k_in[:, cols]).astype(BF)
        kvs[:, (2 * g + 1) * HD : (2 * g + 2) * HD] = dot(hot[...], v_in[:, cols]).astype(BF)
    kvr[mine, :] = kvs[mine, :]
    pl.semaphore_wait(bar, len(friends))
    for j in range(1, NDP):
        kv_copy(j).start()

    q_cp.wait()
    g_cp.wait()

    def send_rows(g, carry):
        cols = pl.ds(pl.multiple_of(g * GW, GW), GW)
        qgs[g, :, 0:GW] = dot(hot[...], q_in[:, cols]).astype(BF)
        qgs[g, :, GW : 2 * GW] = dot(hot[...], g_in[:, cols]).astype(BF)
        qgr[g, mine, :] = qgs[g, mine, :]
        for j in range(1, NDP):
            qg_copy(g, j).start()
        return carry

    lax.fori_loop(0, KH, send_rows, 0)

    q_pos = place_ref[...]
    own_doc = doc_ref[0:1, pl.ds(pl.multiple_of(c * T, T), T)].astype(F32).astype(BF)
    q_doc = dot(jnp.broadcast_to(own_doc, (8, T)), nat[...])[0:1]

    def mask(o, carry):
        at = lax.rem(c - o + 16, 16)
        row = doc_ref[0:1, pl.ds(pl.multiple_of(at * T, T), T)].astype(F32)
        k_doc = jnp.broadcast_to(row, (T, T)).T
        ahead = jnp.where(o == 0, rows - q_pos, 0)
        ahead = jnp.where(o <= c, ahead, 1)
        bias[chunk(o), :] = jnp.where((k_doc == q_doc) & (ahead <= 0), 0.0, NEG)
        return carry

    lax.fori_loop(0, NCH, mask, 0)

    for j in range(1, NDP):
        kv_copy(j).wait_recv()
    for g in range(KH):
        cols = slice(2 * g * HD, 2 * (g + 1) * HD)
        kv[g, 0:T, :] = dot(nat[...], kvr[:, cols]).astype(BF)
        for j in (1, 2):
            x_copy(g, j).start()

    def pass_on(g):
        for j in (1, 2):
            x_copy(g, j).wait_recv()
        for j in (1, 2, 3):
            for b in (0, 1):
                y_copy(g, j, b).start()

    for g in range(3):
        pass_on(g)

    def attend(g):
        for j in range(1, NDP):
            qg_copy(g, j).wait_recv()
        for j in (1, 2, 3):
            for b in (0, 1):
                y_copy(g, j, b).wait_recv()
        keys, values = kv[g, :, 0:HD], kv[g, :, HD : 2 * HD]
        kt[...] = keys.T
        vt[...] = values.T
        query = jnp.concatenate([qgr[g, :, h * HD : (h + 1) * HD] for h in range(GS)], axis=0)
        grad = jnp.concatenate(
            [qgr[g, :, GW + h * HD : GW + (h + 1) * HD] for h in range(GS)], axis=0
        )
        scores = dot(keys, query, NT) * SCALE2 + jnp.concatenate([bias[...]] * GS, axis=1)
        weights = jnp.exp2(scores - jnp.max(scores, axis=0, keepdims=True))
        probs = weights * (1.0 / jnp.sum(weights, axis=0, keepdims=True))
        probs_b = probs.astype(BF)
        out = dot(vt[...], probs_b).astype(BF)
        prob_grad = dot(values, grad, NT)
        delta = jnp.sum(out.astype(F32) * grad.T.astype(F32), axis=0, keepdims=True)
        dscore = (probs * (prob_grad - delta)).astype(BF)
        dq = (dot(kt[...], dscore) * SCALE).astype(BF)
        out, dq = out.T, dq.T
        for h in range(GS):
            ods[g, :, h * HD : (h + 1) * HD] = out[h * T : (h + 1) * T]
            ods[g, :, GW + h * HD : GW + (h + 1) * HD] = dq[h * T : (h + 1) * T]
        dkv[g, :, 0:HD] = (dot(dscore, query) * SCALE).astype(BF)
        dkv[g, :, HD : 2 * HD] = dot(probs_b, grad).astype(BF)
        odr[g, mine, :] = ods[g, mine, :]
        for j in (1, 2, 3):
            for b in (0, 1):
                yr_copy(g, j, b).start()
        for j in range(1, NDP):
            od_copy(g, j).start()

    def add_y(g):
        for k in range(3):
            acc[g, k] = dkv[g, 4 * k * T : (4 * k + 1) * T, :].astype(F32)
        for j in (1, 2, 3):
            turn = (y + j) // 4
            for b in (0, 1):
                yr_copy(g, j, b).wait_recv()
                acc[g, turn + b] += yrec[g, j - 1, b].astype(F32)
        for j in (1, 2):
            xs[g, j - 1] = acc[g, j].astype(BF)
            xr_copy(g, j).start()

    def add_x(g):
        total = acc[g, 0]
        for j in (1, 2):
            xr_copy(g, j).wait_recv()
            total += xrec[g, j - 1].astype(F32)
        zks[g] = dot(nat_t[...], total.astype(BF)).astype(BF)
        zkr[g, mine, :] = zks[g, mine, :]
        for j in range(1, NDP):
            zk_copy(g, j).start()

    def home_copies(g):
        cols = pl.ds(pl.multiple_of(g * GW, GW), GW)
        return (
            pltpu.make_async_copy(home.at[g, :, 0:GW], out_hbm.at[:, cols], out_sem.at[g, 0]),
            pltpu.make_async_copy(home.at[g, :, GW : 2 * GW], dq_hbm.at[:, cols], out_sem.at[g, 1]),
        )

    def come_home(g):
        for j in range(1, NDP):
            od_copy(g, j).wait_recv()
        home[g] = dot(hot_t[...], odr[g]).astype(BF)
        for cp in home_copies(g):
            cp.start()

    def turn(t, carry):
        @pl.when(t < KH)
        def _():
            attend(t)

        @pl.when(t == 0)
        def _():
            pass_on(3)

        @pl.when((t >= 1) & (t <= KH))
        def _():
            add_y(t - 1)

        @pl.when(t >= 2)
        def _():
            add_x(t - 2)
            come_home(t - 2)

        return carry

    lax.fori_loop(0, KH + 2, turn, 0)

    for g in range(KH):
        for j in range(1, NDP):
            zk_copy(g, j).wait_recv()
        grads = dot(hot_t[...], zkr[g]).astype(BF)
        gk[:, g * HD : (g + 1) * HD] = grads[:, 0:HD]
        gv[:, g * HD : (g + 1) * HD] = grads[:, HD : 2 * HD]
    gk_cp = pltpu.make_async_copy(gk, dk_hbm, in_sem.at[0])
    gv_cp = pltpu.make_async_copy(gv, dv_hbm, in_sem.at[1])
    gk_cp.start()
    gv_cp.start()

    for j in range(1, NDP):
        kv_copy(j).wait_send()

    def drain(g, carry):
        for j in range(1, NDP):
            qg_copy(g, j).wait_send()
            od_copy(g, j).wait_send()
            zk_copy(g, j).wait_send()
        for j in (1, 2):
            x_copy(g, j).wait_send()
            xr_copy(g, j).wait_send()
        for j in (1, 2, 3):
            for b in (0, 1):
                y_copy(g, j, b).wait_send()
                yr_copy(g, j, b).wait_send()
        for cp in home_copies(g):
            cp.wait()
        return carry

    lax.fori_loop(0, KH, drain, 0)
    gk_cp.wait()
    gv_cp.wait()


def body(query_rows, key_rows, value_rows, grad_out, send_order, recv_place, doc_ids):
    vm = pltpu.VMEM
    dma = pltpu.SemaphoreType.DMA
    hbm = pl.BlockSpec(memory_space=pl.ANY)
    vmem = pl.BlockSpec(memory_space=pltpu.VMEM)
    wide, thin = (T, KH * GW), (T, KH * HD)
    return pl.pallas_call(
        kernel,
        out_shape=tuple(jax.ShapeDtypeStruct(s, BF) for s in (wide, wide, thin, thin)),
        in_specs=[hbm] * 4 + [vmem] * 3,
        out_specs=(hbm,) * 4,
        scratch_shapes=[
            vm(wide, BF), vm(wide, BF), vm(thin, BF), vm(thin, BF),
            vm((T, T), BF), vm((T, T), BF), vm((T, T), BF), vm((T, T), BF),
            vm((T, 2 * KH * HD), BF), vm((T, 2 * KH * HD), BF),
            vm((KH, T, 2 * GW), BF), vm((KH, T, 2 * GW), BF),
            vm((KH, W, 2 * HD), BF), vm((W, T), F32), vm((HD, W), BF), vm((HD, W), BF),
            vm((KH, T, 2 * GW), BF), vm((KH, T, 2 * GW), BF),
            vm((KH, W, 2 * HD), BF), vm((KH, 3, 2, T, 2 * HD), BF),
            vm((KH, 3, T, 2 * HD), F32), vm((KH, 2, T, 2 * HD), BF), vm((KH, 2, T, 2 * HD), BF),
            vm((KH, T, 2 * HD), BF), vm((KH, T, 2 * HD), BF),
            vm((KH, T, 2 * GW), BF), vm(thin, BF), vm(thin, BF),
            dma((4,)), dma((KH, 2)), dma((NDP,)), dma((NDP,)),
            dma((KH, NDP)), dma((KH, NDP)), dma((KH, 3)), dma((KH, 3)),
            dma((KH, 4, 2)), dma((KH, 4, 2)), dma((KH, NDP)), dma((KH, NDP)),
            dma((KH, 4, 2)), dma((KH, 4, 2)), dma((KH, 3)), dma((KH, 3)),
            dma((KH, NDP)), dma((KH, NDP)),
        ],
        compiler_params=pltpu.CompilerParams(
            collective_id=0, has_side_effects=True, vmem_limit_bytes=60 * 2**20
        ),
    )(
        query_rows, key_rows, value_rows, grad_out,
        send_order.reshape(1, T), recv_place.reshape(1, T), doc_ids,
    )


def solution(mesh):
    rows = P(("dp", "ctx"), None)
    return jax.shard_map(
        body,
        mesh=mesh,
        in_specs=(rows,) * 4 + (P("dp", "ctx", None),) * 2 + (P("dp", None),),
        out_specs=(rows,) * 4,
        check_vma=False,
    )
```

time: 399 us -> 86.2 us (0.22)
  waiting for transfers between devices: 171 us -> 0 us
  Pallas kernels: 0 us -> 80.3 us
  matrix products: 77.2 us -> 0 us
  local copies, waits for them, and re-layouts: 72.2 us -> 5.01 us
  starting transfers between devices: 43.6 us -> 0 us
  other arithmetic: 18 us -> 0 us
  between operations: 14 us -> 0.65 us
    reduce_scatter x2 -> x0, waiting for transfers between devices: 112 us -> none  [the longest x1 69.9 us: body(): lax.psum_scatter(key_parts.reshape(seq_len, -1), 'ctx', scatter_dimension...]
    pallas_call x0 -> x1, Pallas kernels: none -> 80.3 us  [body(): pl.pallas_call(kernel, out_shape=tuple((jax.ShapeDtypeStruct(s, BF) for s...]
    dot_general x28 -> x0, matrix products: 77.2 us -> none  [the longest x4 27.3 us: output_term(): jnp.einsum('kgrj,jkd->rkgd', weights.astype(jnp.bfloat16), value_block, p...]
    all_to_all x8 -> x0, starting transfers between devices: 43.4 us -> none  [the longest x1 6.81 us: body(): lax.all_to_all(key_rows[order_row], 'dp', split_axis=0, concat_axis=0, ti...]
    all_to_all x8 -> x0, waiting for transfers between devices: 37.4 us -> none  [the longest x1 12.9 us: body(): lax.all_to_all(grad_out[order_row], 'dp', split_axis=0, concat_axis=0, ti...]
    gather x16 -> x0, local copies, waits for them, and re-layouts: 28 us -> none  [the longest x4 7.33 us: body(): return tuple((member[order_inverse] for member in all_back))]
    all_gather x2 -> x0, waiting for transfers between devices: 21.9 us -> none  [the longest x1 21.9 us: body(): lax.all_gather(value_local, 'ctx', axis=0, tiled=True)]
    unnamed x28 -> x10, local copies, waits for them, and re-layouts: 15.9 us -> 5.01 us
  transfers between devices with their start and end apart: 12 -> 0, of which waited for: 8 -> 0; matrix products, arithmetic and copies ran while one was open for 15% -> 0% of each run, Pallas kernels for 0% -> 0%
where the time goes in v1:
time: 86.2 us; the launch traced here: 85.9 us
  Pallas kernels  80.3 us (93%)
  local copies, waits for them, and re-layouts  5.01 us (6%)
    pallas_call x1, Pallas kernels, body(): pl.pallas_call(kernel, out_shape=tuple((jax.ShapeDtypeStruct(s, BF) for s...  80.3 us
    unnamed x10, local copies, waits for them, and re-layouts  5.01 us

profile of v1, /device:TPU:1, one launch (start us, length us, event | category | flops | bytes accessed | tf_op | source)
XLA Modules:
  0.0 85.9 jit_solution(14358715201402199285)
XLA Ops:
  0.6 80.3 %shard_map.102 = (bf16[128,4096]{1,0:T(8,128)(2,1)}, bf16[128,4096]{1,0:T(8,128)(2,1)}, bf16[128,512]{1,0:T(8,128)(2,1)}, bf16[128,512]{1,0:T(8,128)(2,1)}) custom-call(bf16[128,4096]{1,0:T(8,128)(2,1)} %q_hbm.1, bf16[128,512]{1,0:T(8,128)(2,1)} %k_hbm.1, bf16[128,512]{1,0:T(8,128)(2,1)} %v_hbm.1, bf16[128,4096]{1,0:T(8,128)(2,1)} %g_hbm.1, ...), custom_call_target="tpu_custom_call" | custom-call | tf_op jit(solution)/shard_map/pallas_call | solution.py:319
  80.9 0.0 copy-start
  80.9 2.4 %copy.15 = bf16[128,4096]{1,0:T(8,128)(2,1)} copy(bf16[128,4096]{1,0:T(8,128)(2,1)} %get-tuple-element.8) | data formatting | bytes 2097152
  83.3 0.0 copy-done
  83.3 0.0 copy-start.2
  83.3 1.0 %copy.16 = bf16[128,4096]{1,0:T(8,128)(2,1)} copy(bf16[128,4096]{1,0:T(8,128)(2,1)S(1)} %copy-done) | data formatting | bytes 2097152
  84.3 0.1 copy-done.2
  84.3 0.0 copy-start.1
  84.3 0.7 copy.17
  85.0 0.3 copy-done.1
  85.3 0.7 copy.18
Async XLA Ops:
  80.9 2.4 %copy-start = (bf16[128,4096]{1,0:T(8,128)(2,1)S(1)}, bf16[128,4096]{1,0:T(8,128)(2,1)}, u32[]{:S(2)}) copy-start(bf16[128,4096]{1,0:T(8,128)(2,1)} %get-tuple-element.9) | copy-start | bytes 3145732
  83.3 1.0 %copy-start.2 = (bf16[128,512]{1,0:T(8,128)(2,1)S(1)}, bf16[128,512]{1,0:T(8,128)(2,1)}, u32[]{:S(2)}) copy-start(bf16[128,512]{1,0:T(8,128)(2,1)} %get-tuple-element.10) | copy-start | bytes 393220
  84.3 1.0 %copy-start.1 = (bf16[128,512]{1,0:T(8,128)(2,1)S(1)}, bf16[128,512]{1,0:T(8,128)(2,1)}, u32[]{:S(2)}) copy-start(bf16[128,512]{1,0:T(8,128)(2,1)} %get-tuple-element.11) | copy-start | bytes 393220

commit v2 on v1

--- a/solution.py
+++ b/solution.py
@@ -21,6 +21,9 @@
 NEG = -1e30
 NT = (((1,), (1,)), ((), ()))
 NN = (((1,), (0,)), ((), ()))
+Y_MSGS = ((1, 0), (2, 0), (3, 0), (1, 1), (3, 1))
+Y_WAIT = tuple(m for m in Y_MSGS if m != (2, 0))
+LAG = 1
 
 
 def dot(a, b, dims=NN):
@@ -29,11 +32,11 @@
 
 def kernel(
     q_hbm, k_hbm, v_hbm, g_hbm, order_ref, place_ref, doc_ref,
-    out_hbm, dq_hbm, dk_hbm, dv_hbm,
-    q_in, g_in, k_in, v_in, hot, hot_t, nat, nat_t,
+    odr, zkr,
+    q_in, g_in, k_in, v_in, hot, nat, nat_t,
     kvs, kvr, qgs, qgr, kv, bias, kt, vt,
-    ods, odr, dkv, yrec, acc, xs, xrec, zks, zkr, home, gk, gv,
-    in_sem, out_sem, kv_ss, kv_rs, qg_ss, qg_rs, x_ss, x_rs, y_ss, y_rs,
+    ods, dkv, y2s, yrec, x6rec, acc, xs, xrec, zks,
+    in_sem, own_sem, kv_ss, kv_rs, qg_ss, qg_rs, x_ss, x_rs, y_ss, y_rs,
     od_ss, od_rs, yr_ss, yr_rs, xr_ss, xr_rs, zk_ss, zk_rs,
 ):
     d = lax.axis_index("dp")
@@ -63,10 +66,8 @@
         cp.start()
 
     rows = lax.broadcasted_iota(I32, (T, T), 0)
-    hot_t32 = (rows == order_ref[...]).astype(F32)
+    hot[...] = (rows == order_ref[...]).astype(F32).T.astype(BF)
     nat32 = (rows == place_ref[...]).astype(F32)
-    hot_t[...] = hot_t32.astype(BF)
-    hot[...] = hot_t32.T.astype(BF)
     nat[...] = nat32.astype(BF)
     nat_t[...] = nat32.T.astype(BF)
 
@@ -102,8 +103,9 @@
         return pl.ds(pl.multiple_of(o * T, T), T)
 
     def x_copy(g, j):
-        return rcopy(
-            kv.at[g, chunk(0)], kv.at[g, chunk(4 * j)], x_ss.at[g, j], x_rs.at[g, j], x_at(j)
+        src, dst, to = ((0, 4, 1), (0, 8, 2), (2, 6, 1))[j - 1]
+        return rcopy(
+            kv.at[g, chunk(src)], kv.at[g, chunk(dst)], x_ss.at[g, j], x_rs.at[g, j], x_at(to)
         )
 
     def y_copy(g, j, b):
@@ -114,15 +116,23 @@
         )
 
     def yr_copy(g, j, b):
-        return rcopy(
-            dkv.at[g, chunk(j + 4 * b)], yrec.at[g, j - 1, b],
-            yr_ss.at[g, j, b], yr_rs.at[g, j, b], y_at(-j),
+        src = y2s.at[g] if (j, b) == (2, 0) else dkv.at[g, chunk(j + 4 * b)]
+        return rcopy(
+            src, yrec.at[g, j - 1, b], yr_ss.at[g, j, b], yr_rs.at[g, j, b], y_at(-j)
         )
 
     def xr_copy(g, j):
-        return rcopy(
-            xs.at[g, j - 1], xrec.at[g, j - 1], xr_ss.at[g, j], xr_rs.at[g, j], x_at(-j)
-        )
+        if j == 3:
+            src, dst, to = dkv.at[g, chunk(6)], x6rec.at[g], 1
+        else:
+            src, dst, to = xs.at[g, j - 1], xrec.at[g, j - 1], j
+        return rcopy(src, dst, xr_ss.at[g, j], xr_rs.at[g, j], x_at(-to))
+
+    def own_od(g):
+        return pltpu.make_async_copy(ods.at[g, mine], odr.at[g, mine], own_sem.at[g, 0])
+
+    def own_zk(g):
+        return pltpu.make_async_copy(zks.at[g, mine], zkr.at[g, mine], own_sem.at[g, 1])
 
     k_cp.wait()
     v_cp.wait()
@@ -172,22 +182,38 @@
         for j in (1, 2):
             x_copy(g, j).start()
 
-    def pass_on(g):
+    def early(g):
+        for j in (1, 2, 3):
+            pl.when(y + j < 4)(y_copy(g, j, 0).start)
+
+    def late(g):
         for j in (1, 2):
             x_copy(g, j).wait_recv()
         for j in (1, 2, 3):
-            for b in (0, 1):
-                y_copy(g, j, b).start()
-
-    for g in range(3):
-        pass_on(g)
+            pl.when(y + j >= 4)(y_copy(g, j, 0).start)
+        for j in (1, 3):
+            y_copy(g, j, 1).start()
+
+    def relay(g):
+        y_copy(g, 2, 0).wait_recv()
+        x_copy(g, 3).start()
+
+    early(0)
+    early(1)
+    late(0)
+    early(2)
+    late(1)
+    early(3)
+    late(2)
+    late(3)
+    relay(0)
 
     def attend(g):
         for j in range(1, NDP):
             qg_copy(g, j).wait_recv()
-        for j in (1, 2, 3):
-            for b in (0, 1):
-                y_copy(g, j, b).wait_recv()
+        for j, b in Y_WAIT:
+            y_copy(g, j, b).wait_recv()
+        x_copy(g, 3).wait_recv()
         keys, values = kv[g, :, 0:HD], kv[g, :, HD : 2 * HD]
         kt[...] = keys.T
         vt[...] = values.T
@@ -210,21 +236,26 @@
             ods[g, :, GW + h * HD : GW + (h + 1) * HD] = dq[h * T : (h + 1) * T]
         dkv[g, :, 0:HD] = (dot(dscore, query) * SCALE).astype(BF)
         dkv[g, :, HD : 2 * HD] = dot(probs_b, grad).astype(BF)
-        odr[g, mine, :] = ods[g, mine, :]
-        for j in (1, 2, 3):
-            for b in (0, 1):
-                yr_copy(g, j, b).start()
+        xr_copy(g, 3).start()
+        for j, b in Y_WAIT:
+            yr_copy(g, j, b).start()
+        own_od(g).start()
         for j in range(1, NDP):
             od_copy(g, j).start()
+
+    def add_relayed(g):
+        xr_copy(g, 3).wait_recv()
+        there = dkv[g, 2 * T : 3 * T, :].astype(F32) + x6rec[g].astype(F32)
+        y2s[g] = there.astype(BF)
+        yr_copy(g, 2, 0).start()
 
     def add_y(g):
         for k in range(3):
             acc[g, k] = dkv[g, 4 * k * T : (4 * k + 1) * T, :].astype(F32)
-        for j in (1, 2, 3):
+        for j, b in Y_MSGS:
             turn = (y + j) // 4
-            for b in (0, 1):
-                yr_copy(g, j, b).wait_recv()
-                acc[g, turn + b] += yrec[g, j - 1, b].astype(F32)
+            yr_copy(g, j, b).wait_recv()
+            acc[g, turn + b] += yrec[g, j - 1, b].astype(F32)
         for j in (1, 2):
             xs[g, j - 1] = acc[g, j].astype(BF)
             xr_copy(g, j).start()
@@ -235,56 +266,21 @@
             xr_copy(g, j).wait_recv()
             total += xrec[g, j - 1].astype(F32)
         zks[g] = dot(nat_t[...], total.astype(BF)).astype(BF)
-        zkr[g, mine, :] = zks[g, mine, :]
+        own_zk(g).start()
         for j in range(1, NDP):
             zk_copy(g, j).start()
-
-    def home_copies(g):
-        cols = pl.ds(pl.multiple_of(g * GW, GW), GW)
-        return (
-            pltpu.make_async_copy(home.at[g, :, 0:GW], out_hbm.at[:, cols], out_sem.at[g, 0]),
-            pltpu.make_async_copy(home.at[g, :, GW : 2 * GW], dq_hbm.at[:, cols], out_sem.at[g, 1]),
-        )
-
-    def come_home(g):
-        for j in range(1, NDP):
-            od_copy(g, j).wait_recv()
-        home[g] = dot(hot_t[...], odr[g]).astype(BF)
-        for cp in home_copies(g):
-            cp.start()
 
     def turn(t, carry):
         @pl.when(t < KH)
         def _():
+            pl.when(t < KH - 1)(lambda: relay(t + 1))
             attend(t)
 
-        @pl.when(t == 0)
-        def _():
-            pass_on(3)
-
-        @pl.when((t >= 1) & (t <= KH))
-        def _():
-            add_y(t - 1)
-
-        @pl.when(t >= 2)
-        def _():
-            add_x(t - 2)
-            come_home(t - 2)
-
+        for step, lag in ((add_relayed, LAG), (add_y, LAG + 1), (add_x, LAG + 2)):
+            pl.when((t >= lag) & (t < KH + lag))(lambda step=step, lag=lag: step(t - lag))
         return carry
 
-    lax.fori_loop(0, KH + 2, turn, 0)
-
-    for g in range(KH):
-        for j in range(1, NDP):
-            zk_copy(g, j).wait_recv()
-        grads = dot(hot_t[...], zkr[g]).astype(BF)
-        gk[:, g * HD : (g + 1) * HD] = grads[:, 0:HD]
-        gv[:, g * HD : (g + 1) * HD] = grads[:, HD : 2 * HD]
-    gk_cp = pltpu.make_async_copy(gk, dk_hbm, in_sem.at[0])
-    gv_cp = pltpu.make_async_copy(gv, dv_hbm, in_sem.at[1])
-    gk_cp.start()
-    gv_cp.start()
+    lax.fori_loop(0, KH + LAG + 2, turn, 0)
 
     for j in range(1, NDP):
         kv_copy(j).wait_send()
@@ -292,22 +288,29 @@
     def drain(g, carry):
         for j in range(1, NDP):
             qg_copy(g, j).wait_send()
-            od_copy(g, j).wait_send()
-            zk_copy(g, j).wait_send()
-        for j in (1, 2):
+            od_copy(g, j).wait()
+            zk_copy(g, j).wait()
+        for j in (1, 2, 3):
             x_copy(g, j).wait_send()
             xr_copy(g, j).wait_send()
-        for j in (1, 2, 3):
-            for b in (0, 1):
-                y_copy(g, j, b).wait_send()
-                yr_copy(g, j, b).wait_send()
-        for cp in home_copies(g):
-            cp.wait()
+        for j, b in Y_MSGS:
+            y_copy(g, j, b).wait_send()
+            yr_copy(g, j, b).wait_send()
+        own_od(g).wait()
+        own_zk(g).wait()
         return carry
 
     lax.fori_loop(0, KH, drain, 0)
-    gk_cp.wait()
-    gv_cp.wait()
+
+
+def home(order_ref, od_ref, zk_ref, out_ref, dq_ref, dk_ref, dv_ref):
+    rows = lax.broadcasted_iota(I32, (T, T), 0)
+    back = (rows == order_ref[...]).astype(F32).astype(BF)
+    out_ref[...] = dot(back, od_ref[0, :, 0:GW]).astype(BF)
+    dq_ref[...] = dot(back, od_ref[0, :, GW : 2 * GW]).astype(BF)
+    grads = dot(back, zk_ref[0]).astype(BF)
+    dk_ref[...] = grads[:, 0:HD]
+    dv_ref[...] = grads[:, HD : 2 * HD]
 
 
 def body(query_rows, key_rows, value_rows, grad_out, send_order, recv_place, doc_ids):
@@ -316,35 +319,51 @@
     hbm = pl.BlockSpec(memory_space=pl.ANY)
     vmem = pl.BlockSpec(memory_space=pltpu.VMEM)
     wide, thin = (T, KH * GW), (T, KH * HD)
-    return pl.pallas_call(
+    order = send_order.reshape(1, T)
+    rows_back, keys_back = pl.pallas_call(
         kernel,
-        out_shape=tuple(jax.ShapeDtypeStruct(s, BF) for s in (wide, wide, thin, thin)),
+        out_shape=(
+            jax.ShapeDtypeStruct((KH, T, 2 * GW), BF),
+            jax.ShapeDtypeStruct((KH, T, 2 * HD), BF),
+        ),
         in_specs=[hbm] * 4 + [vmem] * 3,
-        out_specs=(hbm,) * 4,
+        out_specs=(hbm,) * 2,
         scratch_shapes=[
             vm(wide, BF), vm(wide, BF), vm(thin, BF), vm(thin, BF),
-            vm((T, T), BF), vm((T, T), BF), vm((T, T), BF), vm((T, T), BF),
+            vm((T, T), BF), vm((T, T), BF), vm((T, T), BF),
             vm((T, 2 * KH * HD), BF), vm((T, 2 * KH * HD), BF),
             vm((KH, T, 2 * GW), BF), vm((KH, T, 2 * GW), BF),
             vm((KH, W, 2 * HD), BF), vm((W, T), F32), vm((HD, W), BF), vm((HD, W), BF),
-            vm((KH, T, 2 * GW), BF), vm((KH, T, 2 * GW), BF),
-            vm((KH, W, 2 * HD), BF), vm((KH, 3, 2, T, 2 * HD), BF),
+            vm((KH, T, 2 * GW), BF), vm((KH, W, 2 * HD), BF),
+            vm((KH, T, 2 * HD), BF), vm((KH, 3, 2, T, 2 * HD), BF), vm((KH, T, 2 * HD), BF),
             vm((KH, 3, T, 2 * HD), F32), vm((KH, 2, T, 2 * HD), BF), vm((KH, 2, T, 2 * HD), BF),
-            vm((KH, T, 2 * HD), BF), vm((KH, T, 2 * HD), BF),
-            vm((KH, T, 2 * GW), BF), vm(thin, BF), vm(thin, BF),
+            vm((KH, T, 2 * HD), BF),
             dma((4,)), dma((KH, 2)), dma((NDP,)), dma((NDP,)),
-            dma((KH, NDP)), dma((KH, NDP)), dma((KH, 3)), dma((KH, 3)),
+            dma((KH, NDP)), dma((KH, NDP)), dma((KH, 4)), dma((KH, 4)),
             dma((KH, 4, 2)), dma((KH, 4, 2)), dma((KH, NDP)), dma((KH, NDP)),
-            dma((KH, 4, 2)), dma((KH, 4, 2)), dma((KH, 3)), dma((KH, 3)),
+            dma((KH, 4, 2)), dma((KH, 4, 2)), dma((KH, 4)), dma((KH, 4)),
             dma((KH, NDP)), dma((KH, NDP)),
         ],
         compiler_params=pltpu.CompilerParams(
-            collective_id=0, has_side_effects=True, vmem_limit_bytes=60 * 2**20
+            collective_id=0, has_side_effects=True, vmem_limit_bytes=56 * 2**20
         ),
     )(
         query_rows, key_rows, value_rows, grad_out,
-        send_order.reshape(1, T), recv_place.reshape(1, T), doc_ids,
+        order, recv_place.reshape(1, T), doc_ids,
     )
+    return pl.pallas_call(
+        home,
+        grid=(KH,),
+        out_shape=tuple(jax.ShapeDtypeStruct(s, BF) for s in (wide, wide, thin, thin)),
+        in_specs=[
+            pl.BlockSpec((1, T), lambda g: (0, 0)),
+            pl.BlockSpec((1, T, 2 * GW), lambda g: (g, 0, 0)),
+            pl.BlockSpec((1, T, 2 * HD), lambda g: (g, 0, 0)),
+        ],
+        out_specs=tuple(
+            pl.BlockSpec((T, n), lambda g: (0, g)) for n in (GW, GW, HD, HD)
+        ),
+    )(order, rows_back, keys_back)
 
 
 def solution(mesh):

time: 86.2 us -> 76.8 us (0.89)
  local copies, waits for them, and re-layouts: 5.01 us -> 0 us
  Pallas kernels: 80.3 us -> 75.9 us
    unnamed x10 -> x0, local copies, waits for them, and re-layouts: 5.01 us -> none
    pallas_call x1 -> x2, Pallas kernels: 80.3 us -> 75.9 us  [the longest x1 71.7 us: body(): pl.pallas_call(kernel, out_shape=(jax.ShapeDtypeStruct((KH, T, 2 * GW), B...]
where the time goes in v2:
time: 76.8 us; the launch traced here: 76.5 us
  Pallas kernels  75.9 us (99%)
    pallas_call x1, Pallas kernels, body(): pl.pallas_call(kernel, out_shape=(jax.ShapeDtypeStruct((KH, T, 2 * GW), B...  71.7 us
    pallas_call x1, Pallas kernels, body(): pl.pallas_call(home, grid=(KH,), out_shape=tuple((jax.ShapeDtypeStruct(s,...  4.24 us

profile of v2, /device:TPU:1, one launch (start us, length us, event | category | flops | bytes accessed | tf_op | source)
XLA Modules:
  0.0 76.5 jit_solution(7878297708154663552)
XLA Ops:
  0.6 71.7 %shard_map.102 = (bf16[4,128,2048]{2,1,0:T(8,128)(2,1)}, bf16[4,128,256]{2,1,0:T(8,128)(2,1)}) custom-call(bf16[128,4096]{1,0:T(8,128)(2,1)} %q_hbm.1, bf16[128,512]{1,0:T(8,128)(2,1)} %k_hbm.1, bf16[128,512]{1,0:T(8,128)(2,1)} %v_hbm.1, bf16[128,4096]{1,0:T(8,128)(2,1)} %g_hbm.1, s32[1,128]{1,0:T(1,128)} %bitcast.2, s32[1,128]{1,0:T(1,128)} %bitcast.4, ...), custom_call_target="tpu_custom_call" | custom-call | tf_op jit(solution)/shard_map/pallas_call | solution.py:323
  72.3 4.2 %shard_map.103 = (bf16[128,4096]{1,0:T(8,128)(2,1)}, bf16[128,4096]{1,0:T(8,128)(2,1)}, bf16[128,512]{1,0:T(8,128)(2,1)}, bf16[128,512]{1,0:T(8,128)(2,1)}) custom-call(s32[1,128]{1,0:T(1,128)} %bitcast.3, bf16[4,128,2048]{2,1,0:T(8,128)(2,1)} %get-tuple-element.6.od_ref, bf16[4,128,256]{2,1,0:T(8,128)(2,1)} %get-tuple-element.7.zk_ref), custom_call_target="tpu_custom_call" | custom-call | tf_op jit(solution)/shard_map/pallas_call | solution.py:354

commit v3 on v2

v3 whole, which is shorter than its diff:
```python
import jax
import jax.numpy as jnp
from jax import lax
from jax.experimental import pallas as pl
from jax.experimental.pallas import tpu as pltpu
from jax.sharding import PartitionSpec as P

BF, F32, I32 = jnp.bfloat16, jnp.float32, jnp.int32
MESH = pl.DeviceIdType.MESH
HD = 128
KH = 4
GS = 8
T = 128
NDP = 8
SHARE = T // NDP
NCH = 9
W = NCH * T
GW = GS * HD
SCALE = HD**-0.5
SCALE2 = SCALE * 1.4426950408889634
NEG = -1e30
NT = (((1,), (1,)), ((), ()))
NN = (((1,), (0,)), ((), ()))
Y_MSGS = ((1, 0), (2, 0), (3, 0), (1, 1), (3, 1))
Y_WAIT = tuple(m for m in Y_MSGS if m != (2, 0))
LAG = 1


def dot(a, b, dims=NN):
    return lax.dot_general(a, b, dims, preferred_element_type=F32)


def kernel(
    q_hbm, k_hbm, v_hbm, g_hbm, order_hbm, place_hbm, doc_hbm,
    odr, zkr,
    q_in, g_in, k_in, v_in, hot, nat, nat_t,
    kvs, kvr, qgs, qgr, kv, bias, kt, vt,
    ods, dkv, y2s, yrec, x6rec, acc, xs, xrec, zks,
    order_ref, place_ref, doc_ref, in_sem, own_sem, sent, kv_rs, qg_rs, x_rs, x6_rs, y_rs, y2_rs,
    od_rs, yr_rs, xr_rs, xr6_rs, zk_rs,
):
    d = lax.axis_index("dp")
    c = lax.axis_index("ctx")
    x, y = c // 4, c % 4

    def group_at(j):
        return (lax.rem(d + j, NDP), c)

    def x_at(j):
        return (d, lax.rem(x + j + 4, 4) * 4 + y)

    def y_at(j):
        return (d, x * 4 + lax.rem(y + j + 4, 4))

    bar = pltpu.get_barrier_semaphore()
    friends = [group_at(j) for j in range(1, NDP)]
    friends += [x_at(j) for j in range(1, 4)] + [y_at(j) for j in range(1, 4)]
    for f in friends:
        pl.semaphore_signal(bar, 1, device_id=f, device_id_type=MESH)

    pairs = (
        (order_hbm, order_ref), (k_hbm, k_in), (v_hbm, v_in), (place_hbm, place_ref),
        (doc_hbm, doc_ref), (q_hbm, q_in), (g_hbm, g_in),
    )
    arrivals = [pltpu.make_async_copy(a, b, in_sem.at[n]) for n, (a, b) in enumerate(pairs)]
    for cp in arrivals:
        cp.start()

    rows = lax.broadcasted_iota(I32, (T, T), 0)
    arrivals[0].wait()
    hot[...] = (rows == order_ref[...]).astype(F32).T.astype(BF)
    mine = pl.ds(pl.multiple_of(d * SHARE, SHARE), SHARE)

    def part(j):
        return pl.ds(pl.multiple_of(lax.rem(d + j, NDP) * SHARE, SHARE), SHARE)

    def rcopy(src, dst, ss, rs, to):
        return pltpu.make_async_remote_copy(
            src_ref=src, dst_ref=dst, send_sem=ss, recv_sem=rs, device_id=to, device_id_type=MESH
        )

    def a2a(src, dst, sem, rs, j):
        return rcopy(src.at[part(j)], dst.at[mine], sent.at[sem], rs, group_at(j))

    def kv_copy(j):
        return a2a(kvs, kvr, 0, kv_rs.at[0], j)

    def qg_copy(g, j):
        return a2a(qgs.at[g], qgr.at[g], 1, qg_rs.at[g], j)

    def od_copy(g, j):
        return a2a(ods.at[g], odr.at[g], 2, od_rs.at[0], j)

    def zk_copy(g, j):
        return a2a(zks.at[g], zkr.at[g], 3, zk_rs.at[0], j)

    def landed(ref, rs):
        rcopy(ref, ref, sent.at[0], rs, group_at(1)).wait_recv()

    def left(ref, sem):
        rcopy(ref, ref, sent.at[sem], kv_rs.at[0], group_at(1)).wait_send()

    def chunk(o):
        return pl.ds(pl.multiple_of(o * T, T), T)

    def x_copy(g, j):
        src, dst, to = ((0, 4, 1), (0, 8, 2), (2, 6, 1))[j - 1]
        rs = (x6_rs if j == 3 else x_rs).at[g]
        return rcopy(kv.at[g, chunk(src)], kv.at[g, chunk(dst)], sent.at[4], rs, x_at(to))

    def y_copy(g, j, b):
        src = 4 * ((y + j) // 4 + b)
        rs = (y2_rs if (j, b) == (2, 0) else y_rs).at[g]
        return rcopy(
            kv.at[g, chunk(src)], kv.at[g, chunk(j + 4 * b)], sent.at[5], rs, y_at(j)
        )

    def yr_copy(g, j, b):
        src = y2s.at[g] if (j, b) == (2, 0) else dkv.at[g, chunk(j + 4 * b)]
        return rcopy(src, yrec.at[g, chunk(Y_MSGS.index((j, b)))], sent.at[6], yr_rs.at[g], y_at(-j))

    def xr_copy(g, j):
        if j == 3:
            return rcopy(dkv.at[g, chunk(6)], x6rec.at[g], sent.at[7], xr6_rs.at[g], x_at(-1))
        return rcopy(
            xs.at[g, chunk(j - 1)], xrec.at[g, chunk(j - 1)], sent.at[7], xr_rs.at[g], x_at(-j)
        )

    def own_od():
        return pltpu.make_async_copy(ods.at[:, mine], odr.at[:, mine], own_sem.at[0])

    def own_zk():
        return pltpu.make_async_copy(zks.at[:, mine], zkr.at[:, mine], own_sem.at[1])

    arrivals[1].wait()
    arrivals[2].wait()
    for g in range(KH):
        cols = slice(g * HD, (g + 1) * HD)
        kvs[:, 2 * g * HD : (2 * g + 1) * HD] = dot(hot[...], k_in[:, cols]).astype(BF)
        kvs[:, (2 * g + 1) * HD : (2 * g + 2) * HD] = dot(hot[...], v_in[:, cols]).astype(BF)
    kvr[mine, :] = kvs[mine, :]
    pl.semaphore_wait(bar, len(friends))
    for j in range(1, NDP):
        kv_copy(j).start()

    arrivals[5].wait()
    arrivals[6].wait()

    def send_rows(g, carry):
        cols = pl.ds(pl.multiple_of(g * GW, GW), GW)
        qgs[g, :, 0:GW] = dot(hot[...], q_in[:, cols]).astype(BF)
        qgs[g, :, GW : 2 * GW] = dot(hot[...], g_in[:, cols]).astype(BF)
        qgr[g, mine, :] = qgs[g, mine, :]
        for j in range(1, NDP):
            qg_copy(g, j).start()
        return carry

    lax.fori_loop(0, KH, send_rows, 0)

    arrivals[3].wait()
    arrivals[4].wait()
    nat32 = (rows == place_ref[...]).astype(F32)
    nat[...] = nat32.astype(BF)
    nat_t[...] = nat32.T.astype(BF)
    q_pos = place_ref[...]
    own_doc = doc_ref[0:1, pl.ds(pl.multiple_of(c * T, T), T)].astype(F32).astype(BF)
    q_doc = dot(jnp.broadcast_to(own_doc, (8, T)), nat[...])[0:1]

    def mask(o, carry):
        at = lax.rem(c - o + 16, 16)
        row = doc_ref[0:1, pl.ds(pl.multiple_of(at * T, T), T)].astype(F32)
        k_doc = jnp.broadcast_to(row, (T, T)).T
        ahead = jnp.where(o == 0, rows - q_pos, 0)
        ahead = jnp.where(o <= c, ahead, 1)
        bias[chunk(o), :] = jnp.where((k_doc == q_doc) & (ahead <= 0), 0.0, NEG)
        return carry

    lax.fori_loop(0, NCH, mask, 0)

    others = pl.ds(0, T - SHARE)
    landed(kvr.at[others], kv_rs.at[0])
    for g in range(KH):
        cols = slice(2 * g * HD, 2 * (g + 1) * HD)
        kv[g, 0:T, :] = dot(nat[...], kvr[:, cols]).astype(BF)
        for j in (1, 2):
            x_copy(g, j).start()

    def early(g):
        for j in (1, 2, 3):
            pl.when(y + j < 4)(y_copy(g, j, 0).start)

    def late(g):
        landed(kv.at[g, pl.ds(0, 2 * T)], x_rs.at[g])
        for j in (1, 2, 3):
            pl.when(y + j >= 4)(y_copy(g, j, 0).start)
        for j in (1, 3):
            y_copy(g, j, 1).start()

    def relay(g):
        landed(kv.at[g, pl.ds(0, T)], y2_rs.at[g])
        x_copy(g, 3).start()

    early(0)
    early(1)
    late(0)
    early(2)
    late(1)
    early(3)
    late(2)
    late(3)
    relay(0)

    def attend(g):
        landed(qgr.at[g, others], qg_rs.at[g])
        landed(kv.at[g, pl.ds(0, 4 * T)], y_rs.at[g])
        landed(kv.at[g, pl.ds(0, T)], x6_rs.at[g])
        keys, values = kv[g, :, 0:HD], kv[g, :, HD : 2 * HD]
        kt[...] = keys.T
        vt[...] = values.T
        query = jnp.concatenate([qgr[g, :, h * HD : (h + 1) * HD] for h in range(GS)], axis=0)
        grad = jnp.concatenate(
            [qgr[g, :, GW + h * HD : GW + (h + 1) * HD] for h in range(GS)], axis=0
        )
        scores = dot(keys, query, NT) * SCALE2 + jnp.concatenate([bias[...]] * GS, axis=1)
        weights = jnp.exp2(scores - jnp.max(scores, axis=0, keepdims=True))
        probs = weights * (1.0 / jnp.sum(weights, axis=0, keepdims=True))
        probs_b = probs.astype(BF)
        out = dot(vt[...], probs_b).astype(BF)
        prob_grad = dot(values, grad, NT)
        delta = jnp.sum(out.astype(F32) * grad.T.astype(F32), axis=0, keepdims=True)
        dscore = (probs * (prob_grad - delta)).astype(BF)
        dq = (dot(kt[...], dscore) * SCALE).astype(BF)
        out, dq = out.T, dq.T
        for h in range(GS):
            ods[g, :, h * HD : (h + 1) * HD] = out[h * T : (h + 1) * T]
            ods[g, :, GW + h * HD : GW + (h + 1) * HD] = dq[h * T : (h + 1) * T]
        dkv[g, :, 0:HD] = (dot(dscore, query) * SCALE).astype(BF)
        dkv[g, :, HD : 2 * HD] = dot(probs_b, grad).astype(BF)
        xr_copy(g, 3).start()
        for j, b in Y_WAIT:
            yr_copy(g, j, b).start()
        for j in range(1, NDP):
            od_copy(g, j).start()

    def add_relayed(g):
        landed(x6rec.at[g], xr6_rs.at[g])
        there = dkv[g, 2 * T : 3 * T, :].astype(F32) + x6rec[g].astype(F32)
        y2s[g] = there.astype(BF)
        yr_copy(g, 2, 0).start()

    def add_y(g):
        for k in range(3):
            acc[g, k] = dkv[g, 4 * k * T : (4 * k + 1) * T, :].astype(F32)
        landed(yrec.at[g], yr_rs.at[g])
        for n, (j, b) in enumerate(Y_MSGS):
            acc[g, (y + j) // 4 + b] += yrec[g, n * T : (n + 1) * T, :].astype(F32)
        for j in (1, 2):
            xs[g, (j - 1) * T : j * T, :] = acc[g, j].astype(BF)
            xr_copy(g, j).start()

    def add_x(g):
        landed(xrec.at[g], xr_rs.at[g])
        total = acc[g, 0]
        for j in (1, 2):
            total += xrec[g, (j - 1) * T : j * T, :].astype(F32)
        zks[g] = dot(nat_t[...], total.astype(BF)).astype(BF)
        for j in range(1, NDP):
            zk_copy(g, j).start()

    def turn(t, carry):
        @pl.when(t < KH)
        def _():
            pl.when(t < KH - 1)(lambda: relay(t + 1))
            attend(t)

        for step, lag in ((add_relayed, LAG), (add_y, LAG + 1), (add_x, LAG + 2)):
            pl.when((t >= lag) & (t < KH + lag))(lambda step=step, lag=lag: step(t - lag))
        return carry

    lax.fori_loop(0, KH + LAG + 2, turn, 0)

    own_od().start()
    own_zk().start()
    left(kvs.at[others], 0)
    left(qgs.at[:, others], 1)
    left(ods.at[:, others], 2)
    left(zks.at[:, others], 3)
    left(kv.at[:, pl.ds(0, 3 * T)], 4)
    left(yrec, 5)
    left(yrec, 6)
    left(kv.at[:, pl.ds(0, 3 * T)], 7)
    landed(odr.at[:, others], od_rs.at[0])
    landed(zkr.at[:, others], zk_rs.at[0])
    own_od().wait()
    own_zk().wait()


def home(order_ref, od_hbm, zk_hbm, out_hbm, dq_hbm, dk_hbm, dv_hbm, od, zk, res, gk, gv, sem):
    def come(g):
        return pltpu.make_async_copy(od_hbm.at[g], od.at[g], sem.at[g])

    def leave(g):
        cols = pl.ds(g * GW, GW)
        return (
            pltpu.make_async_copy(res.at[g, :, pl.ds(0, GW)], out_hbm.at[:, cols], sem.at[KH + g]),
            pltpu.make_async_copy(res.at[g, :, pl.ds(GW, GW)], dq_hbm.at[:, cols], sem.at[2 * KH + g]),
        )

    zk_cp = pltpu.make_async_copy(zk_hbm, zk, sem.at[3 * KH])
    for g in range(KH):
        come(g).start()
    zk_cp.start()
    rows = lax.broadcasted_iota(I32, (T, T), 0)
    back = (rows == order_ref[...]).astype(F32).astype(BF)
    for g in range(KH):
        come(g).wait()
        res[g] = dot(back, od[g]).astype(BF)
        for cp in leave(g):
            cp.start()
    zk_cp.wait()
    for g in range(KH):
        grads = dot(back, zk[g]).astype(BF)
        gk[:, g * HD : (g + 1) * HD] = grads[:, 0:HD]
        gv[:, g * HD : (g + 1) * HD] = grads[:, HD : 2 * HD]
    ends = [pltpu.make_async_copy(gk, dk_hbm, sem.at[3 * KH + 1])]
    ends.append(pltpu.make_async_copy(gv, dv_hbm, sem.at[3 * KH + 2]))
    for cp in ends:
        cp.start()
    for g in range(KH):
        for cp in leave(g):
            cp.wait()
    for cp in ends:
        cp.wait()


def body(query_rows, key_rows, value_rows, grad_out, send_order, recv_place, doc_ids):
    vm = pltpu.VMEM
    dma = pltpu.SemaphoreType.DMA
    hbm = pl.BlockSpec(memory_space=pl.ANY)
    vmem = pl.BlockSpec(memory_space=pltpu.VMEM)
    wide, thin = (T, KH * GW), (T, KH * HD)
    order = send_order.reshape(1, T)
    rows_back, keys_back = pl.pallas_call(
        kernel,
        out_shape=(
            jax.ShapeDtypeStruct((KH, T, 2 * GW), BF),
            jax.ShapeDtypeStruct((KH, T, 2 * HD), BF),
        ),
        in_specs=[hbm] * 7,
        out_specs=(hbm,) * 2,
        scratch_shapes=[
            vm(wide, BF), vm(wide, BF), vm(thin, BF), vm(thin, BF),
            vm((T, T), BF), vm((T, T), BF), vm((T, T), BF),
            vm((T, 2 * KH * HD), BF), vm((T, 2 * KH * HD), BF),
            vm((KH, T, 2 * GW), BF), vm((KH, T, 2 * GW), BF),
            vm((KH, W, 2 * HD), BF), vm((W, T), F32), vm((HD, W), BF), vm((HD, W), BF),
            vm((KH, T, 2 * GW), BF), vm((KH, W, 2 * HD), BF),
            vm((KH, T, 2 * HD), BF), vm((KH, 5 * T, 2 * HD), BF), vm((KH, T, 2 * HD), BF),
            vm((KH, 3, T, 2 * HD), F32), vm((KH, 2 * T, 2 * HD), BF), vm((KH, 2 * T, 2 * HD), BF),
            vm((KH, T, 2 * HD), BF),
            vm((1, T), I32), vm((1, T), I32), vm(doc_ids.shape, I32), dma((7,)), dma((2,)),
            dma((8,)), dma((1,)), dma((KH,)), dma((KH,)), dma((KH,)), dma((KH,)), dma((KH,)),
            dma((1,)), dma((KH,)), dma((KH,)), dma((KH,)), dma((1,)),
        ],
        compiler_params=pltpu.CompilerParams(
            collective_id=0, has_side_effects=True, vmem_limit_bytes=56 * 2**20
        ),
    )(
        query_rows, key_rows, value_rows, grad_out,
        order, recv_place.reshape(1, T), doc_ids,
    )
    return pl.pallas_call(
        home,
        out_shape=tuple(jax.ShapeDtypeStruct(s, BF) for s in (wide, wide, thin, thin)),
        in_specs=[vmem, hbm, hbm],
        out_specs=(hbm,) * 4,
        scratch_shapes=[
            vm((KH, T, 2 * GW), BF), vm((KH, T, 2 * HD), BF), vm((KH, T, 2 * GW), BF),
            vm(thin, BF), vm(thin, BF), dma((3 * KH + 3,)),
        ],
        compiler_params=pltpu.CompilerParams(vmem_limit_bytes=16 * 2**20),
    )(order, rows_back, keys_back)


def solution(mesh):
    rows = P(("dp", "ctx"), None)
    return jax.shard_map(
        body,
        mesh=mesh,
        in_specs=(rows,) * 4 + (P("dp", "ctx", None),) * 2 + (P("dp", None),),
        out_specs=(rows,) * 4,
        check_vma=False,
    )
```

time: 76.8 us -> 73.6 us (0.958)
  Pallas kernels: 75.9 us -> 70.2 us
  local copies, waits for them, and re-layouts: 0 us -> 2.54 us
    pallas_call x1, Pallas kernels: 71.7 us -> 67.8 us  [body(): pl.pallas_call(kernel, out_shape=(jax.ShapeDtypeStruct((KH, T, 2 * GW), B...]
    unnamed x0 -> x6, local copies, waits for them, and re-layouts: none -> 2.54 us
    pallas_call x1, Pallas kernels: 4.24 us -> 2.37 us  [body(): pl.pallas_call(home, out_shape=tuple((jax.ShapeDtypeStruct(s, BF) for s i...]
where the time goes in v3:
time: 73.6 us; the launch traced here: 73.4 us
  Pallas kernels  70.2 us (95%)
  local copies, waits for them, and re-layouts  2.54 us (3%)
    pallas_call x1, Pallas kernels, body(): pl.pallas_call(kernel, out_shape=(jax.ShapeDtypeStruct((KH, T, 2 * GW), B...  67.8 us
    unnamed x6, local copies, waits for them, and re-layouts  2.54 us
    pallas_call x1, Pallas kernels, body(): pl.pallas_call(home, out_shape=tuple((jax.ShapeDtypeStruct(s, BF) for s i...  2.37 us

profile of v3, /device:TPU:1, one launch (start us, length us, event | category | flops | bytes accessed | tf_op | source)
XLA Modules:
  0.0 73.4 jit_solution(12974336431485990797)
XLA Ops:
  0.6 0.0 copy-start.2
  0.6 67.8 %shard_map.102 = (bf16[4,128,2048]{2,1,0:T(8,128)(2,1)}, bf16[4,128,256]{2,1,0:T(8,128)(2,1)}) custom-call(bf16[128,4096]{1,0:T(8,128)(2,1)} %q_hbm.1, bf16[128,512]{1,0:T(8,128)(2,1)} %k_hbm.1, bf16[128,512]{1,0:T(8,128)(2,1)} %v_hbm.1, bf16[128,4096]{1,0:T(8,128)(2,1)} %g_hbm.1, s32[1,128]{1,0:T(1,128)} %bitcast.2, s32[1,128]{1,0:T(1,128)} %bitcast.4, ...), custom_call_target="tpu_custom_call" | custom-call | tf_op jit(solution)/shard_map/pallas_call | solution.py:343
  68.4 0.0 copy-done.2
  68.5 0.0 copy-start
  68.5 1.6 %copy-done = bf16[4,128,2048]{2,1,0:T(8,128)(2,1)S(1)} copy-done((bf16[4,128,2048]{2,1,0:T(8,128)(2,1)S(1)}, bf16[4,128,2048]{2,1,0:T(8,128)(2,1)}, u32[]{:S(2)}) %copy-start) | copy-done | bytes 2097176
  70.0 0.0 copy-start.1
  70.0 0.9 %copy-done.1 = bf16[4,128,256]{2,1,0:T(8,128)(2,1)S(1)} copy-done((bf16[4,128,256]{2,1,0:T(8,128)(2,1)S(1)}, bf16[4,128,256]{2,1,0:T(8,128)(2,1)}, u32[]{:S(2)}) %copy-start.1) | copy-done | bytes 262168
  71.0 2.4 %shard_map.103 = (bf16[128,4096]{1,0:T(8,128)(2,1)}, bf16[128,4096]{1,0:T(8,128)(2,1)}, bf16[128,512]{1,0:T(8,128)(2,1)}, bf16[128,512]{1,0:T(8,128)(2,1)}) custom-call(s32[1,128]{1,0:T(1,128)S(1)} %bitcast.3, bf16[4,128,2048]{2,1,0:T(8,128)(2,1)S(1)} %copy-done, bf16[4,128,256]{2,1,0:T(8,128)(2,1)S(1)} %copy-done.1), custom_call_target="tpu_custom_call" | custom-call | tf_op jit(solution)/shard_map/pallas_call | solution.py:372
Async XLA Ops:
  0.6 67.8 %copy-start.2 = (s32[1,1,128]{2,1,0:T(1,128)S(1)}, s32[1,1,128]{2,1,0:T(1,128)}, u32[]{:S(2)}) copy-start(s32[1,1,128]{2,1,0:T(1,128)} %param.11) | copy-start | bytes 1540
  68.5 1.6 %copy-start = (bf16[4,128,2048]{2,1,0:T(8,128)(2,1)S(1)}, bf16[4,128,2048]{2,1,0:T(8,128)(2,1)}, u32[]{:S(2)}) copy-start(bf16[4,128,2048]{2,1,0:T(8,128)(2,1)} %get-tuple-element.6.od_hbm) | copy-start | bytes 6291460
  70.0 0.9 %copy-start.1 = (bf16[4,128,256]{2,1,0:T(8,128)(2,1)S(1)}, bf16[4,128,256]{2,1,0:T(8,128)(2,1)}, u32[]{:S(2)}) copy-start(bf16[4,128,256]{2,1,0:T(8,128)(2,1)} %get-tuple-element.7.zk_hbm) | copy-start | bytes 786436

commit v4 on v3

--- a/solution.py
+++ b/solution.py
@@ -22,8 +22,9 @@
 NT = (((1,), (1,)), ((), ()))
 NN = (((1,), (0,)), ((), ()))
 Y_MSGS = ((1, 0), (2, 0), (3, 0), (1, 1), (3, 1))
-Y_WAIT = tuple(m for m in Y_MSGS if m != (2, 0))
 LAG = 1
+KEYS_DIRECT = ()
+GRADS_DIRECT = (3,)
 
 
 def dot(a, b, dims=NN):
@@ -36,7 +37,7 @@
     q_in, g_in, k_in, v_in, hot, nat, nat_t,
     kvs, kvr, qgs, qgr, kv, bias, kt, vt,
     ods, dkv, y2s, yrec, x6rec, acc, xs, xrec, zks,
-    order_ref, place_ref, doc_ref, in_sem, own_sem, sent, kv_rs, qg_rs, x_rs, x6_rs, y_rs, y2_rs,
+    probs, probs_b, dscore, delta, order_ref, place_ref, doc_ref, in_sem, own_sem, sent, kv_rs, qg_rs, x_rs, x6_rs, y_rs, y2_rs,
     od_rs, yr_rs, xr_rs, xr6_rs, zk_rs,
 ):
     d = lax.axis_index("dp")
@@ -82,8 +83,8 @@
     def a2a(src, dst, sem, rs, j):
         return rcopy(src.at[part(j)], dst.at[mine], sent.at[sem], rs, group_at(j))
 
-    def kv_copy(j):
-        return a2a(kvs, kvr, 0, kv_rs.at[0], j)
+    def kv_copy(g, j):
+        return a2a(kvs.at[g], kvr.at[g], 0, kv_rs.at[g], j)
 
     def qg_copy(g, j):
         return a2a(qgs.at[g], qgr.at[g], 1, qg_rs.at[g], j)
@@ -104,24 +105,44 @@
         return pl.ds(pl.multiple_of(o * T, T), T)
 
     def x_copy(g, j):
-        src, dst, to = ((0, 4, 1), (0, 8, 2), (2, 6, 1))[j - 1]
-        rs = (x6_rs if j == 3 else x_rs).at[g]
-        return rcopy(kv.at[g, chunk(src)], kv.at[g, chunk(dst)], sent.at[4], rs, x_at(to))
+        return rcopy(
+            kv.at[g, chunk(0)], kv.at[g, chunk(4 * j)], sent.at[4], x_rs.at[g], x_at(j)
+        )
+
+    def x_relay(g):
+        return rcopy(kv.at[g, chunk(2)], kv.at[g, chunk(6)], sent.at[8], x6_rs.at[g], x_at(1))
+
+    def y_direct(g):
+        src = 4 * ((y + 2) // 4 + 1)
+        return rcopy(kv.at[g, chunk(src)], kv.at[g, chunk(6)], sent.at[8], x6_rs.at[g], y_at(2))
+
+    def yr_direct(g, j):
+        if j == 6:
+            return rcopy(dkv.at[g, chunk(6)], x6rec.at[g], sent.at[9], xr6_rs.at[g], y_at(-2))
+        at = chunk(Y_MSGS.index((2, 0)))
+        return rcopy(
+            dkv.at[g, chunk(2)], yrec.at[g, at], sent.at[6], yr_rs.at[g], y_at(-2)
+        )
+
+    def grads_direct(g):
+        flag = g < 0
+        for n in GRADS_DIRECT:
+            flag |= g == n
+        return flag
 
     def y_copy(g, j, b):
         src = 4 * ((y + j) // 4 + b)
         rs = (y2_rs if (j, b) == (2, 0) else y_rs).at[g]
-        return rcopy(
-            kv.at[g, chunk(src)], kv.at[g, chunk(j + 4 * b)], sent.at[5], rs, y_at(j)
-        )
+        return rcopy(kv.at[g, chunk(src)], kv.at[g, chunk(j + 4 * b)], sent.at[5], rs, y_at(j))
 
     def yr_copy(g, j, b):
         src = y2s.at[g] if (j, b) == (2, 0) else dkv.at[g, chunk(j + 4 * b)]
         return rcopy(src, yrec.at[g, chunk(Y_MSGS.index((j, b)))], sent.at[6], yr_rs.at[g], y_at(-j))
 
+    def xr_relay(g):
+        return rcopy(dkv.at[g, chunk(6)], x6rec.at[g], sent.at[9], xr6_rs.at[g], x_at(-1))
+
     def xr_copy(g, j):
-        if j == 3:
-            return rcopy(dkv.at[g, chunk(6)], x6rec.at[g], sent.at[7], xr6_rs.at[g], x_at(-1))
         return rcopy(
             xs.at[g, chunk(j - 1)], xrec.at[g, chunk(j - 1)], sent.at[7], xr_rs.at[g], x_at(-j)
         )
@@ -136,12 +157,13 @@
     arrivals[2].wait()
     for g in range(KH):
         cols = slice(g * HD, (g + 1) * HD)
-        kvs[:, 2 * g * HD : (2 * g + 1) * HD] = dot(hot[...], k_in[:, cols]).astype(BF)
-        kvs[:, (2 * g + 1) * HD : (2 * g + 2) * HD] = dot(hot[...], v_in[:, cols]).astype(BF)
-    kvr[mine, :] = kvs[mine, :]
+        kvs[g, :, 0:HD] = dot(hot[...], k_in[:, cols]).astype(BF)
+        kvs[g, :, HD : 2 * HD] = dot(hot[...], v_in[:, cols]).astype(BF)
+    kvr[:, mine, :] = kvs[:, mine, :]
     pl.semaphore_wait(bar, len(friends))
-    for j in range(1, NDP):
-        kv_copy(j).start()
+    for g in range(KH):
+        for j in range(1, NDP):
+            kv_copy(g, j).start()
 
     arrivals[5].wait()
     arrivals[6].wait()
@@ -178,75 +200,95 @@
     lax.fori_loop(0, NCH, mask, 0)
 
     others = pl.ds(0, T - SHARE)
-    landed(kvr.at[others], kv_rs.at[0])
-    for g in range(KH):
-        cols = slice(2 * g * HD, 2 * (g + 1) * HD)
-        kv[g, 0:T, :] = dot(nat[...], kvr[:, cols]).astype(BF)
+    def own(g):
+        landed(kvr.at[g, others], kv_rs.at[g])
+        kv[g, 0:T, :] = dot(nat[...], kvr[g]).astype(BF)
         for j in (1, 2):
             x_copy(g, j).start()
 
     def early(g):
-        for j in (1, 2, 3):
+        for j in (2, 1, 3):
             pl.when(y + j < 4)(y_copy(g, j, 0).start)
 
     def late(g):
         landed(kv.at[g, pl.ds(0, 2 * T)], x_rs.at[g])
-        for j in (1, 2, 3):
+        for j in (2, 1, 3):
             pl.when(y + j >= 4)(y_copy(g, j, 0).start)
         for j in (1, 3):
             y_copy(g, j, 1).start()
+        if g in KEYS_DIRECT:
+            y_direct(g).start()
 
     def relay(g):
         landed(kv.at[g, pl.ds(0, T)], y2_rs.at[g])
-        x_copy(g, 3).start()
-
+        if g not in KEYS_DIRECT:
+            x_relay(g).start()
+
+    own(0)
     early(0)
+    own(1)
+    late(0)
     early(1)
-    late(0)
+    relay(0)
+    late(1)
+    own(2)
     early(2)
-    late(1)
-    early(3)
-    late(2)
-    late(3)
-    relay(0)
+    relay(1)
+
+    def stacked(g, at):
+        return jnp.concatenate(
+            [qgr[g, :, at + h * HD : at + (h + 1) * HD] for h in range(GS)], axis=0
+        )
+
+    def spread(g, at, rows):
+        for h in range(GS):
+            ods[g, :, at + h * HD : at + (h + 1) * HD] = rows[h * T : (h + 1) * T]
 
     def attend(g):
         landed(qgr.at[g, others], qg_rs.at[g])
         landed(kv.at[g, pl.ds(0, 4 * T)], y_rs.at[g])
         landed(kv.at[g, pl.ds(0, T)], x6_rs.at[g])
-        keys, values = kv[g, :, 0:HD], kv[g, :, HD : 2 * HD]
-        kt[...] = keys.T
-        vt[...] = values.T
-        query = jnp.concatenate([qgr[g, :, h * HD : (h + 1) * HD] for h in range(GS)], axis=0)
-        grad = jnp.concatenate(
-            [qgr[g, :, GW + h * HD : GW + (h + 1) * HD] for h in range(GS)], axis=0
-        )
-        scores = dot(keys, query, NT) * SCALE2 + jnp.concatenate([bias[...]] * GS, axis=1)
+        kt[...] = kv[g, :, 0:HD].T
+        vt[...] = kv[g, :, HD : 2 * HD].T
+        scores = dot(kv[g, :, 0:HD], stacked(g, 0), NT) * SCALE2
+        scores += jnp.concatenate([bias[...]] * GS, axis=1)
         weights = jnp.exp2(scores - jnp.max(scores, axis=0, keepdims=True))
-        probs = weights * (1.0 / jnp.sum(weights, axis=0, keepdims=True))
-        probs_b = probs.astype(BF)
-        out = dot(vt[...], probs_b).astype(BF)
-        prob_grad = dot(values, grad, NT)
-        delta = jnp.sum(out.astype(F32) * grad.T.astype(F32), axis=0, keepdims=True)
-        dscore = (probs * (prob_grad - delta)).astype(BF)
-        dq = (dot(kt[...], dscore) * SCALE).astype(BF)
-        out, dq = out.T, dq.T
-        for h in range(GS):
-            ods[g, :, h * HD : (h + 1) * HD] = out[h * T : (h + 1) * T]
-            ods[g, :, GW + h * HD : GW + (h + 1) * HD] = dq[h * T : (h + 1) * T]
-        dkv[g, :, 0:HD] = (dot(dscore, query) * SCALE).astype(BF)
-        dkv[g, :, HD : 2 * HD] = dot(probs_b, grad).astype(BF)
-        xr_copy(g, 3).start()
-        for j, b in Y_WAIT:
+        held = weights * (1.0 / jnp.sum(weights, axis=0, keepdims=True))
+        probs[...] = held
+        probs_b[...] = held.astype(BF)
+        out = dot(vt[...], probs_b[...]).astype(BF)
+        delta[...] = jnp.sum(
+            out.astype(F32) * stacked(g, GW).T.astype(F32), axis=0, keepdims=True
+        )
+        spread(g, 0, out.T)
+
+    def key_grads(g):
+        prob_grad = dot(kv[g, :, HD : 2 * HD], stacked(g, GW), NT)
+        dscore[...] = (probs[...] * (prob_grad - delta[...])).astype(BF)
+        dkv[g, :, 0:HD] = (dot(dscore[...], stacked(g, 0)) * SCALE).astype(BF)
+        dkv[g, :, HD : 2 * HD] = dot(probs_b[...], stacked(g, GW)).astype(BF)
+        pl.when(jnp.logical_not(grads_direct(g)))(xr_relay(g).start)
+
+        @pl.when(grads_direct(g))
+        def _():
+            yr_direct(g, 2).start()
+            yr_direct(g, 6).start()
+
+        for j, b in ((1, 0), (3, 0), (1, 1), (3, 1)):
             yr_copy(g, j, b).start()
+
+    def query_grads(g):
+        spread(g, GW, (dot(kt[...], dscore[...]) * SCALE).astype(BF).T)
         for j in range(1, NDP):
             od_copy(g, j).start()
 
     def add_relayed(g):
-        landed(x6rec.at[g], xr6_rs.at[g])
-        there = dkv[g, 2 * T : 3 * T, :].astype(F32) + x6rec[g].astype(F32)
-        y2s[g] = there.astype(BF)
-        yr_copy(g, 2, 0).start()
+        @pl.when(jnp.logical_not(grads_direct(g)))
+        def _():
+            landed(x6rec.at[g], xr6_rs.at[g])
+            there = dkv[g, 2 * T : 3 * T, :].astype(F32) + x6rec[g].astype(F32)
+            y2s[g] = there.astype(BF)
+            yr_copy(g, 2, 0).start()
 
     def add_y(g):
         for k in range(3):
@@ -254,6 +296,12 @@
         landed(yrec.at[g], yr_rs.at[g])
         for n, (j, b) in enumerate(Y_MSGS):
             acc[g, (y + j) // 4 + b] += yrec[g, n * T : (n + 1) * T, :].astype(F32)
+
+        @pl.when(grads_direct(g))
+        def _():
+            landed(x6rec.at[g], xr6_rs.at[g])
+            acc[g, (y + 2) // 4 + 1] += x6rec[g].astype(F32)
+
         for j in (1, 2):
             xs[g, (j - 1) * T : j * T, :] = acc[g, j].astype(BF)
             xr_copy(g, j).start()
@@ -270,60 +318,67 @@
     def turn(t, carry):
         @pl.when(t < KH)
         def _():
-            pl.when(t < KH - 1)(lambda: relay(t + 1))
             attend(t)
+
+            @pl.when(t == 0)
+            def _():
+                late(2)
+                own(3)
+                early(3)
+
+            @pl.when(t == 1)
+            def _():
+                late(3)
+                relay(2)
+
+            pl.when(t == 2)(lambda: relay(3))
+            key_grads(t)
 
         for step, lag in ((add_relayed, LAG), (add_y, LAG + 1), (add_x, LAG + 2)):
             pl.when((t >= lag) & (t < KH + lag))(lambda step=step, lag=lag: step(t - lag))
+        pl.when(t < KH)(lambda: query_grads(t))
         return carry
 
     lax.fori_loop(0, KH + LAG + 2, turn, 0)
 
     own_od().start()
     own_zk().start()
-    left(kvs.at[others], 0)
+    left(kvs.at[:, others], 0)
     left(qgs.at[:, others], 1)
     left(ods.at[:, others], 2)
     left(zks.at[:, others], 3)
-    left(kv.at[:, pl.ds(0, 3 * T)], 4)
+    left(kv.at[:, pl.ds(0, 2 * T)], 4)
+    left(kv.at[:, pl.ds(0, T)], 8)
+    left(kv.at[:, pl.ds(0, T)], 9)
     left(yrec, 5)
     left(yrec, 6)
-    left(kv.at[:, pl.ds(0, 3 * T)], 7)
+    left(kv.at[:, pl.ds(0, 2 * T)], 7)
     landed(odr.at[:, others], od_rs.at[0])
     landed(zkr.at[:, others], zk_rs.at[0])
     own_od().wait()
     own_zk().wait()
 
 
-def home(order_ref, od_hbm, zk_hbm, out_hbm, dq_hbm, dk_hbm, dv_hbm, od, zk, res, gk, gv, sem):
-    def come(g):
-        return pltpu.make_async_copy(od_hbm.at[g], od.at[g], sem.at[g])
-
+def home(order_ref, od, zk, out_hbm, dq_hbm, dk_hbm, dv_hbm, res, gk, gv, sem):
     def leave(g):
         cols = pl.ds(g * GW, GW)
         return (
-            pltpu.make_async_copy(res.at[g, :, pl.ds(0, GW)], out_hbm.at[:, cols], sem.at[KH + g]),
-            pltpu.make_async_copy(res.at[g, :, pl.ds(GW, GW)], dq_hbm.at[:, cols], sem.at[2 * KH + g]),
-        )
-
-    zk_cp = pltpu.make_async_copy(zk_hbm, zk, sem.at[3 * KH])
-    for g in range(KH):
-        come(g).start()
-    zk_cp.start()
+            pltpu.make_async_copy(res.at[g, :, pl.ds(0, GW)], out_hbm.at[:, cols], sem.at[g]),
+            pltpu.make_async_copy(res.at[g, :, pl.ds(GW, GW)], dq_hbm.at[:, cols], sem.at[KH + g]),
+        )
+
     rows = lax.broadcasted_iota(I32, (T, T), 0)
     back = (rows == order_ref[...]).astype(F32).astype(BF)
     for g in range(KH):
-        come(g).wait()
         res[g] = dot(back, od[g]).astype(BF)
         for cp in leave(g):
             cp.start()
-    zk_cp.wait()
     for g in range(KH):
         grads = dot(back, zk[g]).astype(BF)
         gk[:, g * HD : (g + 1) * HD] = grads[:, 0:HD]
         gv[:, g * HD : (g + 1) * HD] = grads[:, HD : 2 * HD]
-    ends = [pltpu.make_async_copy(gk, dk_hbm, sem.at[3 * KH + 1])]
-    ends.append(pltpu.make_async_copy(gv, dv_hbm, sem.at[3 * KH + 2]))
+    ends = [pltpu.make_async_copy(gk, dk_hbm, sem.at[2 * KH])]
+    ends.append(pltpu.make_async_copy(gv, dv_hbm, sem.at[2 * KH + 1]))
     for cp in ends:
         cp.start()
     for g in range(KH):
@@ -351,32 +406,37 @@
         scratch_shapes=[
             vm(wide, BF), vm(wide, BF), vm(thin, BF), vm(thin, BF),
             vm((T, T), BF), vm((T, T), BF), vm((T, T), BF),
-            vm((T, 2 * KH * HD), BF), vm((T, 2 * KH * HD), BF),
+            vm((KH, T, 2 * HD), BF), vm((KH, T, 2 * HD), BF),
             vm((KH, T, 2 * GW), BF), vm((KH, T, 2 * GW), BF),
             vm((KH, W, 2 * HD), BF), vm((W, T), F32), vm((HD, W), BF), vm((HD, W), BF),
             vm((KH, T, 2 * GW), BF), vm((KH, W, 2 * HD), BF),
             vm((KH, T, 2 * HD), BF), vm((KH, 5 * T, 2 * HD), BF), vm((KH, T, 2 * HD), BF),
             vm((KH, 3, T, 2 * HD), F32), vm((KH, 2 * T, 2 * HD), BF), vm((KH, 2 * T, 2 * HD), BF),
             vm((KH, T, 2 * HD), BF),
+            vm((W, GW), F32), vm((W, GW), BF), vm((W, GW), BF), vm((1, GW), F32),
             vm((1, T), I32), vm((1, T), I32), vm(doc_ids.shape, I32), dma((7,)), dma((2,)),
-            dma((8,)), dma((1,)), dma((KH,)), dma((KH,)), dma((KH,)), dma((KH,)), dma((KH,)),
+            dma((10,)), dma((KH,)), dma((KH,)), dma((KH,)), dma((KH,)), dma((KH,)), dma((KH,)),
             dma((1,)), dma((KH,)), dma((KH,)), dma((KH,)), dma((1,)),
         ],
         compiler_params=pltpu.CompilerParams(
-            collective_id=0, has_side_effects=True, vmem_limit_bytes=56 * 2**20
+            collective_id=0, has_side_effects=True, vmem_limit_bytes=44 * 2**20
         ),
     )(
-        query_rows, key_rows, value_rows, grad_out,
-        order, recv_place.reshape(1, T), doc_ids,
+        *(
+            pltpu.with_memory_space_constraint(a, pltpu.HBM)
+            for a in (
+                query_rows, key_rows, value_rows, grad_out,
+                order, recv_place.reshape(1, T), doc_ids,
+            )
+        )
     )
     return pl.pallas_call(
         home,
         out_shape=tuple(jax.ShapeDtypeStruct(s, BF) for s in (wide, wide, thin, thin)),
-        in_specs=[vmem, hbm, hbm],
+        in_specs=[vmem] * 3,
         out_specs=(hbm,) * 4,
         scratch_shapes=[
-            vm((KH, T, 2 * GW), BF), vm((KH, T, 2 * HD), BF), vm((KH, T, 2 * GW), BF),
-            vm(thin, BF), vm(thin, BF), dma((3 * KH + 3,)),
+            vm((KH, T, 2 * GW), BF), vm(thin, BF), vm(thin, BF), dma((2 * KH + 2,)),
         ],
         compiler_params=pltpu.CompilerParams(vmem_limit_bytes=16 * 2**20),
     )(order, rows_back, keys_back)

time: 73.6 us -> 68.1 us (0.925)
  Pallas kernels: 70.2 us -> 67.4 us
  local copies, waits for them, and re-layouts: 2.54 us -> 0.01 us
    unnamed x6 -> x2, local copies, waits for them, and re-layouts: 2.54 us -> 0.01 us
    pallas_call x1, Pallas kernels: 67.8 us -> 65.6 us  [body(): pl.pallas_call(kernel, out_shape=(jax.ShapeDtypeStruct((KH, T, 2 * GW), B...]
where the time goes in v4:
time: 68.1 us; the launch traced here: 68 us
  Pallas kernels  67.4 us (99%)
    pallas_call x1, Pallas kernels, body(): pl.pallas_call(kernel, out_shape=(jax.ShapeDtypeStruct((KH, T, 2 * GW), B...  65.6 us
    pallas_call x1, Pallas kernels, body(): pl.pallas_call(home, out_shape=tuple((jax.ShapeDtypeStruct(s, BF) for s i...  1.76 us

profile of v4, /device:TPU:1, one launch (start us, length us, event | category | flops | bytes accessed | tf_op | source)
XLA Modules:
  0.0 68.0 jit_solution(17776539503928832176)
XLA Ops:
  0.6 0.0 copy-start
  0.6 65.6 %shard_map.102 = (bf16[4,128,2048]{2,1,0:T(8,128)(2,1)S(1)}, bf16[4,128,256]{2,1,0:T(8,128)(2,1)S(1)}) custom-call(bf16[128,4096]{1,0:T(8,128)(2,1)} %q_hbm.1, bf16[128,512]{1,0:T(8,128)(2,1)} %k_hbm.1, bf16[128,512]{1,0:T(8,128)(2,1)} %v_hbm.1, bf16[128,4096]{1,0:T(8,128)(2,1)} %g_hbm.1, s32[1,128]{1,0:T(1,128)} %bitcast.2, s32[1,128]{1,0:T(1,128)} %bitcast.4, ...), custom_call_target="tpu_custom_call" | custom-call | tf_op jit(solution)/shard_map/pallas_call | solution.py:398
  66.2 0.0 copy-done
  66.3 1.8 %shard_map.103 = (bf16[128,4096]{1,0:T(8,128)(2,1)}, bf16[128,4096]{1,0:T(8,128)(2,1)}, bf16[128,512]{1,0:T(8,128)(2,1)}, bf16[128,512]{1,0:T(8,128)(2,1)}) custom-call(s32[1,128]{1,0:T(1,128)S(1)} %bitcast.3, bf16[4,128,2048]{2,1,0:T(8,128)(2,1)S(1)} %get-tuple-element.6.od, bf16[4,128,256]{2,1,0:T(8,128)(2,1)S(1)} %get-tuple-element.7.zk), custom_call_target="tpu_custom_call" | custom-call | tf_op jit(solution)/shard_map/pallas_call | solution.py:433
Async XLA Ops:
  0.6 65.6 %copy-start = (s32[1,1,128]{2,1,0:T(1,128)S(1)}, s32[1,1,128]{2,1,0:T(1,128)}, u32[]{:S(2)}) copy-start(s32[1,1,128]{2,1,0:T(1,128)} %param.11) | copy-start | bytes 1540

commit v5 on v4

--- a/solution.py
+++ b/solution.py
@@ -180,24 +180,26 @@
     lax.fori_loop(0, KH, send_rows, 0)
 
     arrivals[3].wait()
-    arrivals[4].wait()
     nat32 = (rows == place_ref[...]).astype(F32)
     nat[...] = nat32.astype(BF)
     nat_t[...] = nat32.T.astype(BF)
-    q_pos = place_ref[...]
-    own_doc = doc_ref[0:1, pl.ds(pl.multiple_of(c * T, T), T)].astype(F32).astype(BF)
-    q_doc = dot(jnp.broadcast_to(own_doc, (8, T)), nat[...])[0:1]
-
-    def mask(o, carry):
-        at = lax.rem(c - o + 16, 16)
-        row = doc_ref[0:1, pl.ds(pl.multiple_of(at * T, T), T)].astype(F32)
-        k_doc = jnp.broadcast_to(row, (T, T)).T
-        ahead = jnp.where(o == 0, rows - q_pos, 0)
-        ahead = jnp.where(o <= c, ahead, 1)
-        bias[chunk(o), :] = jnp.where((k_doc == q_doc) & (ahead <= 0), 0.0, NEG)
-        return carry
-
-    lax.fori_loop(0, NCH, mask, 0)
+
+    def masks():
+        arrivals[4].wait()
+        q_pos = place_ref[...]
+        own_doc = doc_ref[0:1, pl.ds(pl.multiple_of(c * T, T), T)].astype(F32).astype(BF)
+        q_doc = dot(jnp.broadcast_to(own_doc, (8, T)), nat[...])[0:1]
+
+        def mask(o, carry):
+            at = lax.rem(c - o + 16, 16)
+            row = doc_ref[0:1, pl.ds(pl.multiple_of(at * T, T), T)].astype(F32)
+            k_doc = jnp.broadcast_to(row, (T, T)).T
+            ahead = jnp.where(o == 0, rows - q_pos, 0)
+            ahead = jnp.where(o <= c, ahead, 1)
+            bias[chunk(o), :] = jnp.where((k_doc == q_doc) & (ahead <= 0), 0.0, NEG)
+            return carry
+
+        lax.fori_loop(0, NCH, mask, 0)
 
     others = pl.ds(0, T - SHARE)
     def own(g):
@@ -229,11 +231,11 @@
     own(1)
     late(0)
     early(1)
+    masks()
     relay(0)
     late(1)
     own(2)
     early(2)
-    relay(1)
 
     def stacked(g, at):
         return jnp.concatenate(
@@ -316,12 +318,17 @@
             zk_copy(g, j).start()
 
     def turn(t, carry):
+        def later(steps):
+            for step, lag in steps:
+                pl.when((t >= lag) & (t < KH + lag))(lambda step=step, lag=lag: step(t - lag))
+
         @pl.when(t < KH)
         def _():
             attend(t)
 
             @pl.when(t == 0)
             def _():
+                relay(1)
                 late(2)
                 own(3)
                 early(3)
@@ -332,10 +339,10 @@
                 relay(2)
 
             pl.when(t == 2)(lambda: relay(3))
-            key_grads(t)
-
-        for step, lag in ((add_relayed, LAG), (add_y, LAG + 1), (add_x, LAG + 2)):
-            pl.when((t >= lag) & (t < KH + lag))(lambda step=step, lag=lag: step(t - lag))
+
+        later(((add_relayed, LAG),))
+        pl.when(t < KH)(lambda: key_grads(t))
+        later(((add_y, LAG + 1),(add_x, LAG + 2),))
         pl.when(t < KH)(lambda: query_grads(t))
         return carry
 

time: 68.1 us -> 66.8 us (0.981)
  Pallas kernels: 67.4 us -> 65.9 us
    pallas_call x1, Pallas kernels: 65.6 us -> 64.1 us  [body(): pl.pallas_call(kernel, out_shape=(jax.ShapeDtypeStruct((KH, T, 2 * GW), B...]
where the time goes in v5:
time: 66.8 us; the launch traced here: 66.5 us
  Pallas kernels  65.9 us (99%)
    pallas_call x1, Pallas kernels, body(): pl.pallas_call(kernel, out_shape=(jax.ShapeDtypeStruct((KH, T, 2 * GW), B...  64.1 us
    pallas_call x1, Pallas kernels, body(): pl.pallas_call(home, out_shape=tuple((jax.ShapeDtypeStruct(s, BF) for s i...  1.76 us

profile of v5, /device:TPU:1, one launch (start us, length us, event | category | flops | bytes accessed | tf_op | source)
XLA Modules:
  0.0 66.5 jit_solution(15249578639237602366)
XLA Ops:
  0.6 0.0 copy-start
  0.6 64.1 %shard_map.102 = (bf16[4,128,2048]{2,1,0:T(8,128)(2,1)S(1)}, bf16[4,128,256]{2,1,0:T(8,128)(2,1)S(1)}) custom-call(bf16[128,4096]{1,0:T(8,128)(2,1)} %q_hbm.1, bf16[128,512]{1,0:T(8,128)(2,1)} %k_hbm.1, bf16[128,512]{1,0:T(8,128)(2,1)} %v_hbm.1, bf16[128,4096]{1,0:T(8,128)(2,1)} %g_hbm.1, s32[1,128]{1,0:T(1,128)} %bitcast.2, s32[1,128]{1,0:T(1,128)} %bitcast.4, ...), custom_call_target="tpu_custom_call" | custom-call | tf_op jit(solution)/shard_map/pallas_call | solution.py:405
  64.8 0.0 copy-done
  64.8 1.8 %shard_map.103 = (bf16[128,4096]{1,0:T(8,128)(2,1)}, bf16[128,4096]{1,0:T(8,128)(2,1)}, bf16[128,512]{1,0:T(8,128)(2,1)}, bf16[128,512]{1,0:T(8,128)(2,1)}) custom-call(s32[1,128]{1,0:T(1,128)S(1)} %bitcast.3, bf16[4,128,2048]{2,1,0:T(8,128)(2,1)S(1)} %get-tuple-element.6.od, bf16[4,128,256]{2,1,0:T(8,128)(2,1)S(1)} %get-tuple-element.7.zk), custom_call_target="tpu_custom_call" | custom-call | tf_op jit(solution)/shard_map/pallas_call | solution.py:440
Async XLA Ops:
  0.6 64.1 %copy-start = (s32[1,1,128]{2,1,0:T(1,128)S(1)}, s32[1,1,128]{2,1,0:T(1,128)}, u32[]{:S(2)}) copy-start(s32[1,1,128]{2,1,0:T(1,128)} %param.11) | copy-start | bytes 1540

commit v6 on v5

--- a/solution.py
+++ b/solution.py
@@ -205,7 +205,7 @@
     def own(g):
         landed(kvr.at[g, others], kv_rs.at[g])
         kv[g, 0:T, :] = dot(nat[...], kvr[g]).astype(BF)
-        for j in (1, 2):
+        for j in (2, 1):
             x_copy(g, j).start()
 
     def early(g):
@@ -304,7 +304,7 @@
             landed(x6rec.at[g], xr6_rs.at[g])
             acc[g, (y + 2) // 4 + 1] += x6rec[g].astype(F32)
 
-        for j in (1, 2):
+        for j in (2, 1):
             xs[g, (j - 1) * T : j * T, :] = acc[g, j].astype(BF)
             xr_copy(g, j).start()
 

time: 66.8 us -> 66.5 us (level)
  no operation moved by 1% of the time
where the time goes in v6:
time: 66.5 us; the launch traced here: 66.2 us
  Pallas kernels  65.5 us (98%)
    pallas_call x1, Pallas kernels, body(): pl.pallas_call(kernel, out_shape=(jax.ShapeDtypeStruct((KH, T, 2 * GW), B...  63.8 us
    pallas_call x1, Pallas kernels, body(): pl.pallas_call(home, out_shape=tuple((jax.ShapeDtypeStruct(s, BF) for s i...  1.76 us

profile of v6, /device:TPU:1, one launch (start us, length us, event | category | flops | bytes accessed | tf_op | source)
XLA Modules:
  0.0 66.2 jit_solution(13709463189077091408)
XLA Ops:
  0.6 0.0 copy-start
  0.6 63.8 %shard_map.102 = (bf16[4,128,2048]{2,1,0:T(8,128)(2,1)S(1)}, bf16[4,128,256]{2,1,0:T(8,128)(2,1)S(1)}) custom-call(bf16[128,4096]{1,0:T(8,128)(2,1)} %q_hbm.1, bf16[128,512]{1,0:T(8,128)(2,1)} %k_hbm.1, bf16[128,512]{1,0:T(8,128)(2,1)} %v_hbm.1, bf16[128,4096]{1,0:T(8,128)(2,1)} %g_hbm.1, s32[1,128]{1,0:T(1,128)} %bitcast.2, s32[1,128]{1,0:T(1,128)} %bitcast.4, ...), custom_call_target="tpu_custom_call" | custom-call | tf_op jit(solution)/shard_map/pallas_call | solution.py:405
  64.4 0.0 copy-done
  64.4 1.8 %shard_map.103 = (bf16[128,4096]{1,0:T(8,128)(2,1)}, bf16[128,4096]{1,0:T(8,128)(2,1)}, bf16[128,512]{1,0:T(8,128)(2,1)}, bf16[128,512]{1,0:T(8,128)(2,1)}) custom-call(s32[1,128]{1,0:T(1,128)S(1)} %bitcast.3, bf16[4,128,2048]{2,1,0:T(8,128)(2,1)S(1)} %get-tuple-element.6.od, bf16[4,128,256]{2,1,0:T(8,128)(2,1)S(1)} %get-tuple-element.7.zk), custom_call_target="tpu_custom_call" | custom-call | tf_op jit(solution)/shard_map/pallas_call | solution.py:440
Async XLA Ops:
  0.6 63.8 %copy-start = (s32[1,1,128]{2,1,0:T(1,128)S(1)}, s32[1,1,128]{2,1,0:T(1,128)}, u32[]{:S(2)}) copy-start(s32[1,1,128]{2,1,0:T(1,128)} %param.11) | copy-start | bytes 1540
